TPU v7x, 128 devices: a whole 4x4x4 slice. The times are simulated.
128 devices in a mesh: dp: 32 (over z_lo, x, y), mp: 4 (over z_hi, core).
Axes of the slice: x: 4, y: 4, z: 4 (z_hi: 2, z_lo: 2; z = z_hi * 2 + z_lo), core: 2. Of those that a mesh axis runs over, the one named last changes fastest.
Arguments:
- image_feats: bfloat16 [16384, 1152], P(('dp', 'mp')), may hold values from -6 to 6
- text_feats: bfloat16 [16384, 1152], P(('dp', 'mp')), may hold values from -6 to 6
- image_proj: bfloat16 [1152, 1152], replicated, may hold values from -0.1875 to 0.1875
- text_proj: bfloat16 [1152, 1152], replicated, may hold values from -0.1875 to 0.1875
- log_scale: float32 [1], replicated, may hold values from 3.6 to 4.3
- logit_bias: float32 [1], replicated, may hold values from -12 to -9
Outputs:
- loss: float32 [1], replicated
- image_proj_grad: float32 [1152, 1152], P(('dp', 'mp'))
- text_proj_grad: float32 [1152, 1152], P(('dp', 'mp'))
- log_scale_grad: float32 [1], replicated
- bias_grad: float32 [1], replicated
All inputs are finite; a program needn't handle non-finite values.
Results may differ from a plain program's by a relative error of at most 0.0035.
Values may be sent and summed in bfloat16 or wider, within the bound.
A program may use at most 128 MiB of HBM per device.

v0:
```python
import jax
import jax.numpy as jnp
from jax import lax
from jax.sharding import PartitionSpec as P


def normalize(features, projection):
    projected = jnp.dot(features, projection, preferred_element_type=jnp.float32)
    row_norm = jnp.sqrt(jnp.sum(projected * projected, axis=-1, keepdims=True) + 1e-06)
    return (projected / row_norm, row_norm)


def unnormalize(unit_rows, row_norm, unit_grad):
    inner_product = jnp.sum(unit_rows * unit_grad, axis=-1, keepdims=True)
    return ((unit_grad - unit_rows * inner_product) / row_norm).astype(jnp.bfloat16)


def pair_terms(cosine, label_signs, logit_scale, bias_value):
    logits = logit_scale * cosine + bias_value
    losses = -jax.nn.log_sigmoid(label_signs * logits)
    pair_grads = -label_signs * jax.nn.sigmoid(-label_signs * logits)
    return (
        jnp.sum(losses),
        jnp.sum(pair_grads * logit_scale * cosine),
        jnp.sum(pair_grads),
        pair_grads.astype(jnp.bfloat16),
    )


def pair_signs(dp_index, mp_index, own_rows, mp_size, dp_size):
    row_ids = dp_index * own_rows * mp_size + jnp.arange(own_rows * mp_size, dtype=jnp.int32)
    column = jnp.arange(own_rows * dp_size, dtype=jnp.int32)
    column_ids = (column // own_rows * mp_size + mp_index) * own_rows + column % own_rows
    return jnp.where(row_ids[:, None] == column_ids[None, :], 1.0, -1.0).astype(jnp.float32)


def per_device(image_feats, text_feats, image_proj, text_proj, log_scale, logit_bias):
    own_rows = image_feats.shape[0]
    dp_size = lax.axis_size("dp")
    mp_size = lax.axis_size("mp")
    dp_index = lax.axis_index("dp")
    mp_index = lax.axis_index("mp")
    image_unit, image_norm = normalize(image_feats, image_proj)
    text_unit, text_norm = normalize(text_feats, text_proj)
    image_half = image_unit.astype(jnp.bfloat16)
    text_half = text_unit.astype(jnp.bfloat16)
    logit_scale = jnp.exp(log_scale[0])
    bias_value = logit_bias[0]
    label_signs = pair_signs(dp_index, mp_index, own_rows, mp_size, dp_size)
    image_group = lax.all_gather(image_half, "mp", axis=0, tiled=True)
    text_loop = lax.all_gather(text_half, "dp", axis=0, tiled=True)
    cosine = jnp.einsum("id,jd->ij", image_group, text_loop, preferred_element_type=jnp.float32)
    loss_part, scale_part, bias_part, half_grads = pair_terms(
        cosine, label_signs, logit_scale, bias_value
    )
    image_terms = logit_scale * jnp.dot(half_grads, text_loop, preferred_element_type=jnp.float32)
    image_grad = lax.psum_scatter(image_terms, "mp", scatter_dimension=0, tiled=True)
    text_grad = lax.psum_scatter(
        logit_scale
        * jnp.einsum("ij,id->jd", half_grads, image_group, preferred_element_type=jnp.float32),
        "dp",
        scatter_dimension=0,
        tiled=True,
    )
    image_dy = unnormalize(image_unit, image_norm, image_grad)
    text_dy = unnormalize(text_unit, text_norm, text_grad)
    image_part = jnp.einsum("rd,re->de", image_feats, image_dy, preferred_element_type=jnp.float32)
    text_part = jnp.einsum("rd,re->de", text_feats, text_dy, preferred_element_type=jnp.float32)
    image_proj_grad, text_proj_grad = (
        lax.psum_scatter(image_part, ("dp", "mp"), scatter_dimension=0, tiled=True),
        lax.psum_scatter(text_part, ("dp", "mp"), scatter_dimension=0, tiled=True),
    )
    loss_sum, scale_sum, bias_sum = lax.psum((loss_part, scale_part, bias_part), ("dp", "mp"))
    batch_total = own_rows * dp_size * mp_size
    return (
        (loss_sum / batch_total).reshape(1),
        image_proj_grad,
        text_proj_grad,
        (scale_sum / batch_total).reshape(1),
        (bias_sum / batch_total).reshape(1),
    )


def solution(mesh):
    return jax.shard_map(
        per_device,
        mesh=mesh,
        in_specs=(P(("dp", "mp"), None), P(("dp", "mp"), None), P(), P(), P(), P()),
        out_specs=(P(), P(("dp", "mp"), None), P(("dp", "mp"), None), P(), P()),
        check_vma=False,
    )
```

profile of v0, /device:TPU:1, one launch (start us, length us, event | category | flops | bytes accessed | tf_op | source)
XLA Modules:
  0.0 681.2 jit_solution(10889926284767577416)
XLA Ops:
  7.2 0.0 copy-start
  7.2 0.0 all-gather.3.cloned.1.call-start
  7.2 1.7 copy-done
  8.9 1.6 multiply_reduce_fusion.4
  10.6 0.8 fusion.25
  11.4 0.0 all-gather.3.cloned.1.call-update
  11.5 0.0 all-gather.5.cloned.1.call-start
  11.5 2.5 multiply_reduce_fusion.3
  14.1 0.0 copy-start.2
  14.1 0.9 fusion.26
  15.0 0.0 all-gather.5.cloned.1.call-update
  15.0 0.0 reduce-scatter.5.cloned.1.call-start
  16.5 20.4 %all-gather.3.cloned.1.call-done = bf16[512,1152]{1,0:T(8,128)(2,1)} async-done(((bf16[128,1152]{1,0:T(8,128)(2,1)}), bf16[512,1152]{1,0:T(8,128)(2,1)}) %all-gather.3.cloned.1.call-update) | async-done | bytes 1179664 | tf_op jit(solution)/shard_map/all_gather | solution.py:50
  36.9 151.4 %all-gather.5.cloned.1.call-done = bf16[4096,1152]{1,0:T(8,128)(2,1)} async-done(((bf16[128,1152]{1,0:T(8,128)(2,1)}), bf16[4096,1152]{1,0:T(8,128)(2,1)}) %all-gather.5.cloned.1.call-update) | async-done | bytes 9437200 | tf_op jit(solution)/shard_map/all_gather | solution.py:51
  188.3 0.0 copy-start.5
  188.3 18.0 %fusion.28 = (f32[]{:T(128)}, f32[]{:T(128)}, f32[]{:T(128)}, f32[512,4096]{1,0:T(8,128)S(1)}) fusion(f32[]{:T(128)} %bitcast.23, f32[]{:T(128)} %bitcast, s32[4096]{0:T(1024)S(1)} %fusion.23, s32[512]{0:T(512)S(1)} %iota_add_fusion, bf16[512,1152]{1,0:T(8,128)(2,1)} %all-gather.3.cloned.1.call-done, bf16[4096,1152]{1,0:T(8,128)(2,1)} %all-gather.5.cloned.1.call-done), kind=kOutput, calls=%fused_computation.53 | convolution fusion | flops 4880072704 | bytes 19023892 | tf_op jit(solution)/shard_map/id,jd->ij/dot_general | solution.py:52
  206.3 0.0 copy-start.7
  206.3 3.4 copy-done.7
  209.7 0.0 copy-done.5
  209.7 0.0 copy-start.6
  209.7 9.3 %convolution_multiply_fusion.1 = f32[512,1152]{1,0:T(8,128)} fusion(bf16[4096,1152]{1,0:T(8,128)(2,1)S(1)} %copy-done.5, f32[]{:T(128)} %bitcast, f32[512,4096]{1,0:T(8,128)S(1)} %get-tuple-element.27, f32[]{:T(128)} %bitcast.24, s32[4096]{0:T(1024)S(1)} %fusion.23, s32[512]{0:T(512)S(1)} %iota_add_fusion), kind=kOutput, calls=%fused_computation.16 | convolution fusion | flops 4855496704 | bytes 20203528 | tf_op jit(solution)/shard_map/dot_general | solution.py:56
  219.0 0.0 reduce-scatter.5.cloned.1.call-update
  219.0 0.0 reduce-scatter.7.cloned.1.call-start
  219.0 0.0 copy-done.6
  219.0 13.7 %convolution_multiply_fusion = f32[4096,1152]{1,0:T(8,128)} fusion(bf16[512,1152]{1,0:T(8,128)(2,1)S(1)} %copy-done.6, f32[]{:T(128)} %bitcast, f32[512,4096]{1,0:T(8,128)} %copy-done.7, f32[]{:T(128)} %bitcast.25, s32[4096]{0:T(1024)S(1)} %fusion.23, s32[512]{0:T(512)S(1)} %iota_add_fusion), kind=kOutput, calls=%fused_computation.1 | convolution fusion | flops 4859625472 | bytes 28461064 | tf_op jit(solution)/shard_map/ij,id->jd/dot_general | solution.py:60
  232.8 0.0 copy-start.3
  232.8 0.0 reduce-scatter.7.cloned.1.call-update
  232.8 0.0 copy-start.4
  232.8 0.3 all-reduce.6.cloned.1.call-start
  233.1 44.8 %reduce-scatter.5.cloned.1.call-done = f32[128,1152]{1,0:T(8,128)} async-done(((f32[512,1152]{1,0:T(8,128)}), f32[128,1152]{1,0:T(8,128)}) %reduce-scatter.5.cloned.1.call-update) | async-done | bytes 589840 | tf_op jit(solution)/shard_map/reduce_scatter | solution.py:57
  277.9 1.3 multiply_reduce_fusion.2
  279.1 0.0 copy-done.3
  279.2 4.4 convolution_bitcast_fusion.1
  283.5 202.4 %reduce-scatter.7.cloned.1.call-done = f32[128,1152]{1,0:T(8,128)} async-done(((f32[4096,1152]{1,0:T(8,128)}), f32[128,1152]{1,0:T(8,128)}) %reduce-scatter.7.cloned.1.call-update) | async-done | bytes 589840 | tf_op jit(solution)/shard_map/reduce_scatter | solution.py:58
  485.9 0.0 copy-done.2
  485.9 1.3 multiply_reduce_fusion.1
  487.2 0.0 copy-done.4
  487.2 0.0 copy-start.1
  487.2 4.7 convolution_bitcast_fusion
  491.9 0.0 all-reduce.6.cloned.1.call-update
  491.9 73.5 %all-reduce.2 = (f32[]{:T(128)}, f32[]{:T(128)}, f32[]{:T(128)}) all-reduce(f32[]{:T(128)} %get-tuple-element.17, f32[]{:T(128)} %get-tuple-element.16, f32[]{:T(128)} %get-tuple-element.15), channel_id=1, replica_groups=mesh['dp'=32,'mp'=4] {'dp','mp'}, use_global_device_ids=true, to_apply=%region_3.4 | all-reduce | flops 3 | bytes 24 | tf_op jit(solution)/shard_map/psum | solution.py:73
  567.3 98.4 %all-reduce.6.cloned.1.call-done = (f32[1152,1152]{0,1:T(8,128)}, f32[1152,1152]{0,1:T(8,128)}) async-done(((f32[1152,1152]{0,1:T(8,128)}, f32[1152,1152]{0,1:T(8,128)}), (f32[1152,1152]{0,1:T(8,128)}, f32[1152,1152]{0,1:T(8,128)})) %all-reduce.6.cloned.1.call-update) | async-done | bytes 10616848
  665.7 2.8 constant_dynamic-slice_fusion
  668.5 1.9 copy.13
  670.5 0.9 copy.14
  671.3 0.0 copy-done.1
  (4 shorter events, 0.0 us)
Async XLA Ops:
  7.2 1.8 copy-start
  7.2 29.7 %all-gather.3.cloned.1.call-start = ((), (), s32[]{:S(2)}) async-start(), calls=%async_computation.2 | async-start | bytes 1474560 | tf_op jit(solution)/shard_map/all_gather | solution.py:50
  11.5 176.8 %all-gather.5.cloned.1.call-start = ((), (), s32[]{:S(2)}) async-start(), calls=%async_computation.3 | async-start | bytes 9732096 | tf_op jit(solution)/shard_map/all_gather | solution.py:51
  14.1 471.9 %copy-start.2 = (f32[128,1152]{1,0:T(8,128)}, f32[128,1152]{1,0:T(8,128)S(1)}, u32[]{:S(2)}) copy-start(f32[128,1152]{1,0:T(8,128)S(1)} %get-tuple-element.26) | copy-start | bytes 1769476
  15.0 262.8 %reduce-scatter.5.cloned.1.call-start = ((), (), s32[]{:S(2)}) async-start(), calls=%async_computation.4 | async-start | bytes 2949120 | tf_op jit(solution)/shard_map/reduce_scatter | solution.py:57
  188.3 21.4 %copy-start.5 = (bf16[4096,1152]{1,0:T(8,128)(2,1)S(1)}, bf16[4096,1152]{1,0:T(8,128)(2,1)}, u32[]{:S(2)}) copy-start(bf16[4096,1152]{1,0:T(8,128)(2,1)} %all-gather.5.cloned.1.call-done) | copy-start | bytes 28311556
  206.3 3.4 copy-start.7
  209.7 9.4 %copy-start.6 = (bf16[512,1152]{1,0:T(8,128)(2,1)S(1)}, bf16[512,1152]{1,0:T(8,128)(2,1)}, u32[]{:S(2)}) copy-start(bf16[512,1152]{1,0:T(8,128)(2,1)} %all-gather.3.cloned.1.call-done) | copy-start | bytes 3538948
  219.0 266.9 %reduce-scatter.7.cloned.1.call-start = ((), (), s32[]{:S(2)}) async-start(), calls=%async_computation.5 | async-start | bytes 19464192 | tf_op jit(solution)/shard_map/reduce_scatter | solution.py:58
  232.8 46.4 %copy-start.3 = (bf16[128,1152]{1,0:T(8,128)(2,1)S(1)}, bf16[128,1152]{1,0:T(8,128)(2,1)}, u32[]{:S(2)}) copy-start(bf16[128,1152]{1,0:T(8,128)(2,1)} %param.6) | copy-start | bytes 884740
  232.8 254.4 %copy-start.4 = (bf16[128,1152]{1,0:T(8,128)(2,1)S(1)}, bf16[128,1152]{1,0:T(8,128)(2,1)}, u32[]{:S(2)}) copy-start(bf16[128,1152]{1,0:T(8,128)(2,1)} %param.7) | copy-start | bytes 884740
  232.8 432.9 %all-reduce.6.cloned.1.call-start = ((), (), s32[]{:S(2)}) async-start(), calls=%async_computation.6 | async-start | bytes 21233664
  487.2 184.1 %copy-start.1 = (bf16[1152,1152]{1,0:T(8,128)(2,1)S(1)}, bf16[1152,1152]{1,0:T(8,128)(2,1)}, u32[]{:S(2)}) copy-start(bf16[1152,1152]{1,0:T(8,128)(2,1)} %param.8) | copy-start | bytes 7962628
Sparse Core Ops, SparseCore 0:
  11.6 25.2 all-gather.2
  38.5 149.7 all-gather.4
  219.1 58.7 reduce-scatter.4
  280.3 205.5 reduce-scatter.6
  492.0 173.6 all-reduce.5
where the time goes:
time: 682 us; the launch traced here: 681 us
  waiting for transfers between devices  517 us (76%)
  blocking collectives  73.5 us (11%)
  matrix products  54.3 us (8%)
  between operations  20.5 us (3%)
  local copies, waits for them, and re-layouts  10.7 us (2%)
    reduce_scatter x1, waiting for transfers between devices, per_device(): lax.psum_scatter(logit_scale * jnp.einsum('ij,id->jd', half_grads, image_...  202 us
    all_gather x1, waiting for transfers between devices, per_device(): text_loop = lax.all_gather(text_half, 'dp', axis=0, tiled=True)  151 us
    unnamed x6, waiting for transfers between devices  98.5 us
    psum x1, blocking collectives, per_device(): lax.psum((loss_part, scale_part, bias_part), ('dp', 'mp'))  73.5 us
    reduce_scatter x1, waiting for transfers between devices, per_device(): lax.psum_scatter(image_terms, 'mp', scatter_dimension=0, tiled=True)  44.8 us
    all_gather x1, waiting for transfers between devices, per_device(): image_group = lax.all_gather(image_half, 'mp', axis=0, tiled=True)  20.4 us
    dot_general x1, matrix products, per_device(): jnp.einsum('id,jd->ij', image_group, text_loop, preferred_element_type=jn...  18 us
    dot_general x1, matrix products, per_device(): jnp.einsum('ij,id->jd', half_grads, image_group, preferred_element_type=j...  13.7 us
  transfers between devices with their start and end apart: 5, of which 5 were waited for; matrix products, arithmetic and copies ran while one was open for 3% of the time, Pallas kernels for 0%

commit v1 on v0

v1 whole, which is shorter than its diff:
```python
import functools

import jax
import jax.numpy as jnp
from jax import lax
from jax.experimental import pallas as pl
from jax.experimental.pallas import tpu as pltpu
from jax.sharding import PartitionSpec as P

MESH = pl.DeviceIdType.MESH
BF16, F32 = jnp.bfloat16, jnp.float32
WIDTH = 1152
OWN = 128
UNIT = 2 * OWN
ROWS = 8 * UNIT
TILE = 512
PART = WIDTH // 3
LOG2E = 1.4426950408889634

UNITS = {(0, 0): 0, (1, 0): 1, (0, 3): 2, (0, 1): 3, (1, 3): 4, (1, 1): 5, (0, 2): 6, (1, 2): 7}
RING_UP = [((0, 0, 0), (0, 3, 0)), ((0, 0, 1), (0, 3, 1)), ((1, 0, 1), (1, 3, 1)), ((0, 3, 1), (0, 2, 1)), ((1, 3, 1), (1, 2, 1))]
RING_DOWN = [((0, 0, 0), (0, 1, 0)), ((0, 0, 1), (0, 1, 1)), ((0, 1, 0), (0, 2, 0)), ((1, 0, 1), (1, 1, 1)), ((1, 1, 0), (1, 2, 0))]
ACROSS = [((0, 0, 0), (1, 0, 0)), ((0, 0, 1), (1, 0, 1)), ((0, 1, 0), (1, 1, 0)), ((0, 3, 0), (1, 3, 0))]
ORDERS = [(0, 1, 2), (1, 2, 0), (2, 0, 1)]


def device(x, y, z, core):
    x, y, z = lax.rem(x, 4), lax.rem(y, 4), lax.rem(z, 4)
    return (lax.rem(z, 2) * 16 + x * 4 + y, lax.div(z, 2) * 2 + core)


def natural_row(x, y, z):
    return 18 * (((z % 2) * 16 + x * 4 + y) * 2 + z // 2)


def fold(v):
    return v[0:8] + v[8:16] + v[16:24] + v[24:32]


def kernel(
    log_scale, logit_bias, image_feats, text_feats, image_proj, text_proj,
    loss_out, image_out, text_out, scale_out, bias_out,
    feats, feats_t, unit, unit_low, other, pairs, pairs_t, proj, inv_norm, wide, perm, sums,
    first_a, first_b, first_c, into_a, into_b, into_c, part_sum, second_out, second_in, third_out, third_own, third_in,
    scalars, last, last_in,
    local_sem, gather_send, gather_recv, unit_send, unit_recv, tile_send, tile_recv,
    first_send, first_recv, second_send, second_recv, third_send, third_recv, scalar_send, scalar_recv, last_sem,
):
    dp, mp = lax.axis_index("dp"), lax.axis_index("mp")
    core = lax.rem(mp, 2)
    x = lax.rem(lax.div(dp, 4), 4)
    y = lax.rem(dp, 4)
    z = lax.div(mp, 2) * 2 + lax.div(dp, 16)
    pos = (x, y, z)
    is_image = core == 0
    sibling = (dp, mp + 1 - 2 * core)

    def along(axis, step):
        moved = [x, y, z]
        moved[axis] = moved[axis] + step
        return device(*moved, core)

    def ring(step):
        return device(jnp.where(is_image, x, x + step), y, jnp.where(is_image, z + step, z), core)

    even = lax.rem(y, 2) == 0
    across = device(x, jnp.where(is_image == even, y + 1, y + 3), z, core)

    def remote(src, dst, send, recv, to):
        return pltpu.make_async_remote_copy(
            src_ref=src, dst_ref=dst, send_sem=send, recv_sem=recv, device_id=to, device_id_type=MESH
        )

    def slot(key):
        dy, dr, half = key
        side = core if half == 0 else 1 - core
        return pl.ds(pl.multiple_of(UNITS[(dy, dr)] * UNIT + side * OWN, OWN), OWN)

    def arrival(key):
        return gather_recv.at[UNITS[key[:2]] * 2 + key[2]]

    own = slot((0, 0, 0))
    own_copy = pltpu.make_async_copy(image_feats, feats.at[own], local_sem.at[0])
    proj_copy = pltpu.make_async_copy(image_proj, proj, local_sem.at[1])

    @pl.when(is_image)
    def _():
        own_copy.start()
        proj_copy.start()

    @pl.when(jnp.logical_not(is_image))
    def _():
        pltpu.make_async_copy(text_feats, feats.at[own], local_sem.at[0]).start()
        pltpu.make_async_copy(text_proj, proj, local_sem.at[1]).start()

    barrier = pltpu.get_barrier_semaphore()
    partners = [along(axis, step) for axis in range(3) for step in (1, 2, 3)] + [sibling]
    for partner in partners:
        pl.semaphore_signal(barrier, inc=1, device_id=partner, device_id_type=MESH)
    pl.semaphore_wait(barrier, len(partners))

    def cross(src):
        return remote(src, feats.at[own], gather_send.at[14], gather_recv.at[1], sibling)

    @pl.when(is_image)
    def _():
        cross(text_feats).start()

    @pl.when(jnp.logical_not(is_image))
    def _():
        cross(image_feats).start()

    own_copy.wait()

    sends = {}
    for index, (path, to) in enumerate(((RING_UP, ring(1)), (RING_DOWN, ring(3)), (ACROSS, across))):
        for step, (source, target) in enumerate(path):
            sends[(index, step)] = remote(
                feats.at[slot(source)], feats.at[slot(target)], gather_send.at[index * 5 + step], arrival(target), to
            )

    def arrived(*key):
        remote(feats.at[slot(key)], feats.at[slot(key)], gather_send.at[0], arrival(key), sibling).wait_recv()

    for index in range(3):
        sends[(index, 0)].start()
    arrived(0, 0, 1)
    for index in range(3):
        sends[(index, 1)].start()
    proj_copy.wait()

    def unit_copy(index):
        rows = pl.ds(pl.multiple_of(index * UNIT, UNIT), UNIT)
        return remote(unit.at[rows], other.at[rows], unit_send.at[index], unit_recv.at[index], sibling)

    def project(index, carry):
        rows = pl.ds(pl.multiple_of(index * UNIT, UNIT), UNIT)
        wide[pl.ds(0, UNIT), :] = jnp.dot(feats[rows, :], proj[...], preferred_element_type=F32)

        def chunk(i, c):
            here = pl.ds(pl.multiple_of(i * 32, 32), 32)
            there = pl.ds(pl.multiple_of(index * UNIT + i * 32, 32), 32)
            raw = wide[here, :]
            inv = 1.0 / jnp.sqrt(jnp.sum(raw * raw, axis=1, keepdims=True) + 1e-06)
            value = raw * inv
            half = value.astype(BF16)
            unit[there, :] = half
            unit_low[there, :] = (value - half.astype(F32)).astype(BF16)
            inv_norm[there, :] = inv
            return c

        lax.fori_loop(0, UNIT // 32, chunk, 0)
        unit_copy(index).start()
        feats_t[:, rows] = feats[rows, :].T
        return carry

    scale = jnp.exp(jnp.full((1, TILE), log_scale[0], F32))
    slope = scale * LOG2E
    offset = jnp.full((1, TILE), logit_bias[0], F32) * LOG2E

    def tile_copy(t, a, b):
        return remote(
            pairs_t.at[t],
            pairs.at[pl.ds(pl.multiple_of(b * TILE, TILE), TILE), pl.ds(pl.multiple_of(a * TILE, TILE), TILE)],
            tile_send.at[t], tile_recv.at[t], sibling,
        )

    def tile_place(t):
        a = jnp.where(t < 4, lax.rem(t, 2), 2 + lax.div(t - 4, 2))
        b = lax.rem(a + core, 2) + jnp.where(t < 2, 0, jnp.where(t < 4, 2, 2 * lax.rem(t, 2)))
        return a, b

    def tile(t, carry):
        a, b = tile_place(t)
        rows = pl.ds(pl.multiple_of(a * TILE, TILE), TILE)
        cols = pl.ds(pl.multiple_of(b * TILE, TILE), TILE)
        wide[pl.ds(0, TILE), pl.ds(0, TILE)] = lax.dot_general(
            unit[rows, :], other[cols, :], (((1,), (1,)), ((), ())), preferred_element_type=F32
        )

        def run(diagonal):
            def chunk(i, acc):
                here = pl.ds(pl.multiple_of(i * 32, 32), 32)
                cosine = wide[here, pl.ds(0, TILE)]
                arg = cosine * slope + offset
                if diagonal:
                    row = i * 32 + lax.broadcasted_iota(jnp.int32, (32, TILE), 0)
                    col = lax.broadcasted_iota(jnp.int32, (32, TILE), 1)
                    sign = jnp.where((row == col) & (col < UNIT), -1.0, 1.0).astype(F32)
                    arg = arg * sign
                up = jnp.exp2(arg)
                whole = 1.0 + up
                inv = pl.reciprocal(whole, approx=True)
                inv = inv * (2.0 - whole * inv)
                grad = up * inv
                loss = jnp.log(whole) + (up - (whole - 1.0)) * inv
                if diagonal:
                    grad = grad * sign
                pairs[pl.ds(pl.multiple_of(a * TILE + i * 32, 32), 32), cols] = grad.astype(BF16)
                return acc[0] + fold(loss), acc[1] + fold(grad * cosine), acc[2] + fold(grad)

            zero = jnp.zeros((8, TILE), F32)
            acc = lax.fori_loop(0, TILE // 32, chunk, (zero, zero, zero))
            for k in range(3):
                sums[k] += acc[k]

        on_diagonal = jnp.logical_and(is_image, t == 0)
        pl.when(on_diagonal)(lambda: run(True))
        pl.when(jnp.logical_not(on_diagonal))(lambda: run(False))
        pairs_t[t] = pairs[rows, cols].T
        tile_copy(t, a, b).start()
        return carry

    sums[...] = jnp.zeros_like(sums)
    project(0, 0)
    arrived(0, 1, 0)
    sends[(1, 2)].start()
    sends[(2, 2)].start()
    arrived(0, 3, 0)
    sends[(2, 3)].start()
    arrived(1, 0, 0)
    arrived(1, 0, 1)
    sends[(0, 2)].start()
    sends[(1, 3)].start()
    arrived(0, 3, 1)
    sends[(0, 3)].start()
    arrived(0, 1, 1)
    lax.fori_loop(1, 4, project, 0)
    arrived(1, 3, 1)
    sends[(0, 4)].start()
    arrived(1, 1, 0)
    sends[(1, 4)].start()
    for index in range(4):
        unit_copy(index).wait_recv()
    lax.fori_loop(0, 2, tile, 0)
    for key in ((0, 2, 0), (0, 2, 1), (1, 1, 1), (1, 3, 0)):
        arrived(*key)
    lax.fori_loop(4, 7, project, 0)
    arrived(1, 2, 0)
    arrived(1, 2, 1)
    project(7, 0)
    for index in range(4, 8):
        unit_copy(index).wait_recv()
    lax.fori_loop(2, 8, tile, 0)

    def scalar_copies(stage):
        if stage == 3:
            return [remote(scalars.at[3, core], scalars.at[3, core], scalar_send.at[9], scalar_recv.at[9], sibling)]
        return [
            remote(
                scalars.at[stage, pos[stage]], scalars.at[stage, pos[stage]],
                scalar_send.at[stage * 3 + step - 1], scalar_recv.at[stage * 3 + step - 1], along(stage, step),
            )
            for step in (1, 2, 3)
        ]

    def scalar_start(stage, value):
        scalars[stage, pos[stage] if stage < 3 else core] = value
        for copy in scalar_copies(stage):
            copy.start()

    def scalar_finish(stage):
        for copy in scalar_copies(stage):
            copy.wait()
        if stage == 3:
            return scalars[3, 0] + scalars[3, 1]
        return (scalars[stage, 0] + scalars[stage, 1]) + (scalars[stage, 2] + scalars[stage, 3])

    lanes = [sums[k][:, 0:128] + sums[k][:, 128:256] + (sums[k][:, 256:384] + sums[k][:, 384:512]) for k in range(3)]
    scalar_start(0, jnp.concatenate(lanes, axis=0))

    for copy in sends.values():
        copy.wait_send()
    cross(text_feats).wait_send()
    for t in range(8):
        tile_copy(t, 0, 0).wait_recv()

    scale_row = jnp.exp(jnp.full((1, 1), log_scale[0], F32))

    def backward(a, carry):
        rows = pl.ds(pl.multiple_of(a * TILE, TILE), TILE)
        wide[pl.ds(0, TILE), :] = jnp.dot(pairs[rows, :], other[...], preferred_element_type=F32)

        def chunk(i, c):
            here = pl.ds(pl.multiple_of(i * 32, 32), 32)
            there = pl.ds(pl.multiple_of(a * TILE + i * 32, 32), 32)
            grad = wide[here, :]
            value = unit[there, :].astype(F32) + unit_low[there, :].astype(F32)
            inner = jnp.sum(value * grad, axis=1, keepdims=True)
            feats[there, :] = ((grad - value * inner) * (inv_norm[there, :] * scale_row)).astype(BF16)
            return c

        lax.fori_loop(0, TILE // 32, chunk, 0)
        return carry

    lax.fori_loop(0, 4, backward, 0)
    scalar_start(1, scalar_finish(0))

    def weight_tile(n, carry):
        cols = pl.ds(pl.multiple_of(n * 256, 256), 256)
        wide[:, cols] = jnp.dot(feats_t[...], feats[:, cols], preferred_element_type=F32)
        return carry

    up = 1 - 2 * core

    def first_copies(p):
        axis = ORDERS[p][0]
        ahead, behind = along(axis, lax.rem(4 + up, 4)), along(axis, lax.rem(4 - up, 4))
        return (
            remote(first_a.at[p], into_a.at[p], first_send.at[p, 0], first_recv.at[p, 0], ahead),
            remote(first_b.at[p], into_b.at[p], first_send.at[p, 1], first_recv.at[p, 1], behind),
            remote(first_c.at[p], into_c.at[p], first_send.at[p, 2], first_recv.at[p, 2], ahead),
        )

    def block(p, step):
        k = lax.rem(pos[ORDERS[p][0]] + 4 + step, 4)
        return pl.ds(pl.multiple_of(k * 288, 288), 288), pl.ds(p * PART, PART)

    def first_start(p):
        columns = pl.ds(p * PART, PART)
        for k1 in range(4):
            for k2 in range(4):
                for k3 in range(4):
                    place = [0, 0, 0]
                    for axis, k in zip(ORDERS[p], (k1, k2, k3)):
                        place[axis] = k
                    perm[pl.ds(k1 * 288 + k2 * 72 + k3 * 18, 18), columns] = wide[pl.ds(natural_row(*place), 18), columns]
        first_a[p] = perm[block(p, 2)].astype(BF16)
        first_b[p] = perm[block(p, -up)].astype(BF16)
        copies = first_copies(p)
        copies[0].start()
        copies[1].start()

    def first_forward(p):
        copies = first_copies(p)
        copies[0].wait_recv()
        first_c[p] = (perm[block(p, up)] + into_a[p].astype(F32)).astype(BF16)
        copies[2].start()

    def second_copies(p):
        return [
            remote(second_out.at[p, step - 1], second_in.at[p, step - 1], second_send.at[p, step - 1],
                   second_recv.at[p, step - 1], along(ORDERS[p][1], step))
            for step in (1, 2, 3)
        ]

    def second_rows(p, step):
        return pl.ds(pl.multiple_of(lax.rem(pos[ORDERS[p][1]] + step, 4) * 72, 8), 72)

    def second_start(p):
        copies = first_copies(p)
        copies[1].wait_recv()
        copies[2].wait_recv()
        part_sum[p] = perm[block(p, 0)] + into_b[p].astype(F32) + into_c[p].astype(F32)
        for step, copy in zip((1, 2, 3), second_copies(p)):
            second_out[p, step - 1, pl.ds(0, 72), :] = part_sum[p, second_rows(p, step), :].astype(BF16)
            copy.start()

    def third_copies(p):
        at = pos[ORDERS[p][2]]
        return [
            remote(third_out.at[p, lax.rem(at + step, 4)], third_in.at[p, step - 1], third_send.at[p, step - 1],
                   third_recv.at[p, step - 1], along(ORDERS[p][2], step))
            for step in (1, 2, 3)
        ]

    def third_start(p):
        total = part_sum[p, second_rows(p, 0), :]
        for step, copy in zip((1, 2, 3), second_copies(p)):
            copy.wait_recv()
            total += second_in[p, step - 1, pl.ds(0, 72), :].astype(F32)
        part_sum[p, pl.ds(0, 72), :] = total
        for k in range(4):
            piece = part_sum[p, pl.ds(18 * k, 18), :]
            third_own[p, k, pl.ds(0, 18), :] = piece
            third_out[p, k, pl.ds(0, 18), :] = piece.astype(BF16)
        for copy in third_copies(p):
            copy.start()

    def third_finish(p):
        total = third_own[p, pos[ORDERS[p][2]], pl.ds(0, 18), :]
        for step, copy in zip((1, 2, 3), third_copies(p)):
            copy.wait_recv()
            total += third_in[p, step - 1, pl.ds(0, 18), :].astype(F32)
        third_own[p, 0, pl.ds(0, 18), :] = total
        columns = pl.ds(p * PART, PART)
        for h in range(2):
            last[h, pl.ds(0, 9), columns] = third_own[p, 0, pl.ds(9 * h, 9), :]

    lax.fori_loop(0, 2, weight_tile, 0)
    first_start(0)
    lax.fori_loop(2, 3, weight_tile, 0)
    first_start(1)
    lax.fori_loop(3, 4, weight_tile, 0)
    first_forward(0)
    wide[:, pl.ds(1024, 128)] = jnp.dot(feats_t[...], feats[:, pl.ds(1024, 128)], preferred_element_type=F32)
    first_start(2)
    first_forward(1)
    scalar_start(2, scalar_finish(1))
    second_start(0)
    first_forward(2)
    second_start(1)
    scalar_start(3, scalar_finish(2))
    third_start(0)
    second_start(2)
    third_start(1)
    totals = scalar_finish(3)
    third_finish(0)
    third_start(2)
    third_finish(1)
    batch = 1.0 / 16384.0
    loss_out[0] = jnp.sum(totals[0:8]) * batch
    scale_out[0] = jnp.sum(totals[8:16] * jnp.exp(jnp.full((8, 128), log_scale[0], F32))) * batch
    bias_out[0] = jnp.sum(totals[16:24]) * batch
    third_finish(2)

    exchange = remote(last.at[1 - core], last_in, last_sem.at[0], last_sem.at[1], sibling)
    exchange.start()
    for p in range(3):
        for copy in first_copies(p) + tuple(second_copies(p)) + tuple(third_copies(p)):
            copy.wait_send()
    for index in range(8):
        unit_copy(index).wait_send()
        tile_copy(index, 0, 0).wait_send()
    exchange.wait()
    rows = pl.ds(0, 9)

    @pl.when(is_image)
    def _():
        image_out[...] = last[0, rows, :]
        text_out[...] = last_in[rows, :]

    @pl.when(jnp.logical_not(is_image))
    def _():
        image_out[...] = last_in[rows, :]
        text_out[...] = last[1, rows, :]


def per_device(image_feats, text_feats, image_proj, text_proj, log_scale, logit_bias):
    smem = pl.BlockSpec(memory_space=pltpu.SMEM)
    vmem = pl.BlockSpec(memory_space=pltpu.VMEM)
    hbm = pl.BlockSpec(memory_space=pl.ANY)
    dma, buffer = pltpu.SemaphoreType.DMA, pltpu.VMEM
    one = jax.ShapeDtypeStruct((1,), F32)
    rows = jax.ShapeDtypeStruct((9, WIDTH), F32)
    loss, image_grad, text_grad, scale_grad, bias_grad = pl.pallas_call(
        kernel,
        out_shape=(one, rows, rows, one, one),
        in_specs=[smem, smem, hbm, hbm, hbm, hbm],
        out_specs=(smem, vmem, vmem, smem, smem),
        scratch_shapes=[
            buffer((ROWS, WIDTH), BF16),
            buffer((WIDTH, ROWS), BF16),
            buffer((ROWS, WIDTH), BF16),
            buffer((ROWS, WIDTH), BF16),
            buffer((ROWS, WIDTH), BF16),
            buffer((ROWS, ROWS), BF16),
            buffer((8, TILE, TILE), BF16),
            buffer((WIDTH, WIDTH), BF16),
            buffer((ROWS, 1), F32),
            buffer((WIDTH, WIDTH), F32),
            buffer((WIDTH, WIDTH), F32),
            buffer((3, 8, TILE), F32),
            *[buffer((3, 288, PART), BF16) for _ in range(6)],
            buffer((3, 288, PART), F32),
            buffer((3, 3, 80, PART), BF16),
            buffer((3, 3, 80, PART), BF16),
            buffer((3, 4, 32, PART), BF16),
            buffer((3, 4, 24, PART), F32),
            buffer((3, 3, 32, PART), BF16),
            buffer((4, 4, 24, 128), F32),
            buffer((2, 16, WIDTH), F32),
            buffer((16, WIDTH), F32),
            dma((2,)),
            dma((15,)), dma((16,)),
            dma((8,)), dma((8,)),
            dma((8,)), dma((8,)),
            dma((3, 3)), dma((3, 3)),
            dma((3, 3)), dma((3, 3)),
            dma((3, 3)), dma((3, 3)),
            dma((10,)), dma((10,)),
            dma((2,)),
        ],
        compiler_params=pltpu.CompilerParams(collective_id=0, has_side_effects=True, vmem_limit_bytes=62 * 2**20),
        name="sigmoid_loss",
    )(log_scale, logit_bias, image_feats, text_feats, image_proj, text_proj)
    return loss, image_grad, text_grad, scale_grad, bias_grad


def solution(mesh):
    return jax.shard_map(
        per_device,
        mesh=mesh,
        in_specs=(P(("dp", "mp"), None), P(("dp", "mp"), None), P(), P(), P(), P()),
        out_specs=(P(), P(("dp", "mp"), None), P(("dp", "mp"), None), P(), P()),
        check_vma=False,
    )
```

time: 682 us -> 120 us (0.18)
  waiting for transfers between devices: 517 us -> 0 us
  Pallas kernels: 0 us -> 109 us
  blocking collectives: 73.5 us -> 0 us
  matrix products: 54.3 us -> 0 us
  between operations: 20.5 us -> 7.21 us
  local copies, waits for them, and re-layouts: 10.7 us -> 3.04 us
    reduce_scatter x2 -> x0, waiting for transfers between devices: 247 us -> none  [the longest x1 202 us: per_device(): lax.psum_scatter(logit_scale * jnp.einsum('ij,id->jd', half_grads, image_...]
    all_gather x2 -> x0, waiting for transfers between devices: 172 us -> none  [the longest x1 151 us: per_device(): text_loop = lax.all_gather(text_half, 'dp', axis=0, tiled=True)]
    pallas_call x0 -> x1, Pallas kernels: none -> 109 us  [per_device(): pl.pallas_call(kernel, out_shape=(one, rows, rows, one, one), in_specs=[s...]
    unnamed x6 -> x0, waiting for transfers between devices: 98.5 us -> none
    psum x1 -> x0, blocking collectives: 73.5 us -> none  [per_device(): lax.psum((loss_part, scale_part, bias_part), ('dp', 'mp'))]
    dot_general x7 -> x0, matrix products: 54.3 us -> none  [the longest x1 18 us: per_device(): jnp.einsum('id,jd->ij', image_group, text_loop, preferred_element_type=jn...]
    unnamed x19 -> x2, local copies, waits for them, and re-layouts: 10.7 us -> 3.04 us
  transfers between devices with their start and end apart: 5 -> 0, of which waited for: 5 -> 0; matrix products, arithmetic and copies ran while one was open for 3% -> 0% of each run, Pallas kernels for 0% -> 0%
where the time goes in v1:
time: 120 us
  Pallas kernels  109 us (91%)
  between operations  7.21 us (6%)
  local copies, waits for them, and re-layouts  3.04 us (3%)
    pallas_call x1, Pallas kernels, per_device(): pl.pallas_call(kernel, out_shape=(one, rows, rows, one, one), in_specs=[s...  109 us
    unnamed x2, local copies, waits for them, and re-layouts  3.04 us

profile of v1, /device:TPU:1, one launch (start us, length us, event | category | flops | bytes accessed | tf_op | source)
XLA Modules:
  0.0 119.6 jit_solution(16981736919914789836)
XLA Ops:
  1.9 109.4 %sigmoid_loss.1 = (f32[1]{0:T(128)}, f32[9,1152]{1,0:T(8,128)}, f32[9,1152]{1,0:T(8,128)}, f32[1]{0:T(128)}, f32[1]{0:T(128)}) custom-call(f32[1]{0:T(128)S(6)} %copy.16.log_scale, f32[1]{0:T(128)S(6)} %copy.17.logit_bias, bf16[128,1152]{1,0:T(8,128)(2,1)} %image_feats.1, bf16[128,1152]{1,0:T(8,128)(2,1)} %text_feats.1, bf16[1152,1152]{1,0:T(8,128)(2,1)} %image_proj.1, ...), custom_call_target="tpu_custom_call" | custom-call | tf_op jit(solution)/shard_map/sigmoid_loss/pallas_call | solution.py:446
  111.9 1.5 %copy.19 = f32[9,1152]{1,0:T(8,128)} copy(f32[9,1152]{1,0:T(8,128)} %get-tuple-element.11) | data formatting | bytes 82944
  113.5 1.5 %copy.20 = f32[9,1152]{1,0:T(8,128)} copy(f32[9,1152]{1,0:T(8,128)} %get-tuple-element.12) | data formatting | bytes 82944

commit v2 on v1

v2 whole, which is shorter than its diff:
```python
import functools

import jax
import jax.numpy as jnp
from jax import lax
from jax.experimental import pallas as pl
from jax.experimental.pallas import tpu as pltpu
from jax.sharding import PartitionSpec as P

MESH = pl.DeviceIdType.MESH
BF16, F32 = jnp.bfloat16, jnp.float32
WIDTH = 1152
OWN = 128
UNIT = 2 * OWN
ROWS = 8 * UNIT
TILE = 512
PART = 128
THIRD = 3 * PART
STEP = 16
LOG2E = 1.4426950408889634

UNITS = {(0, 0): 0, (1, 0): 1, (0, 3): 2, (0, 1): 3, (1, 3): 4, (1, 1): 5, (0, 2): 6, (1, 2): 7}
RING_UP = [((0, 0, 0), (0, 3, 0)), ((0, 0, 1), (0, 3, 1)), ((1, 0, 1), (1, 3, 1)), ((0, 3, 1), (0, 2, 1)), ((1, 3, 1), (1, 2, 1))]
RING_DOWN = [((0, 0, 0), (0, 1, 0)), ((0, 0, 1), (0, 1, 1)), ((0, 1, 0), (0, 2, 0)), ((1, 0, 1), (1, 1, 1)), ((1, 1, 0), (1, 2, 0))]
ACROSS = [((0, 0, 0), (1, 0, 0)), ((0, 0, 1), (1, 0, 1)), ((0, 1, 0), (1, 1, 0)), ((0, 3, 0), (1, 3, 0))]
ORDERS = [(0, 1, 2), (1, 2, 0), (2, 0, 1)]


def device(x, y, z, core):
    x, y, z = lax.rem(x, 4), lax.rem(y, 4), lax.rem(z, 4)
    return (lax.rem(z, 2) * 16 + x * 4 + y, lax.div(z, 2) * 2 + core)


def natural_row(x, y, z):
    return 18 * (((z % 2) * 16 + x * 4 + y) * 2 + z // 2)


def fold(v):
    return v[0:8] + v[8:16]


def kernel(
    log_scale, logit_bias, image_feats, text_feats, image_proj, text_proj,
    loss_out, image_out, text_out, scale_out, bias_out,
    feats, feats_t, unit, unit_low, other, pairs, pairs_t, proj, inv_norm, wide, perm, sums,
    first_a, first_b, into_a, into_b, into_c, part_sum, second_out, second_in, third_own, third_in,
    scalars, last, last_in,
    local_sem, gather_send, gather_recv, unit_send, unit_recv, tile_send, tile_recv,
    first_send, first_recv, second_send, second_recv, third_send, third_recv, scalar_send, scalar_recv, last_sem,
):
    dp, mp = lax.axis_index("dp"), lax.axis_index("mp")
    core = lax.rem(mp, 2)
    x = lax.rem(lax.div(dp, 4), 4)
    y = lax.rem(dp, 4)
    z = lax.div(mp, 2) * 2 + lax.div(dp, 16)
    pos = (x, y, z)
    is_image = core == 0
    sibling = (dp, mp + 1 - 2 * core)

    def along(axis, step):
        moved = [x, y, z]
        moved[axis] = moved[axis] + step
        return device(*moved, core)

    def ring(step):
        return device(jnp.where(is_image, x, x + step), y, jnp.where(is_image, z + step, z), core)

    even = lax.rem(y, 2) == 0
    across = device(x, jnp.where(is_image == even, y + 1, y + 3), z, core)

    def remote(src, dst, send, recv, to):
        return pltpu.make_async_remote_copy(
            src_ref=src, dst_ref=dst, send_sem=send, recv_sem=recv, device_id=to, device_id_type=MESH
        )

    def slot(key):
        dy, dr, half = key
        side = core if half == 0 else 1 - core
        return pl.ds(pl.multiple_of(UNITS[(dy, dr)] * UNIT + side * OWN, OWN), OWN)

    def arrival(key):
        return gather_recv.at[UNITS[key[:2]] * 2 + key[2]]

    own = slot((0, 0, 0))
    own_copy = pltpu.make_async_copy(image_feats, feats.at[own], local_sem.at[0])
    proj_copy = pltpu.make_async_copy(image_proj, proj, local_sem.at[1])

    @pl.when(is_image)
    def _():
        own_copy.start()
        proj_copy.start()

    @pl.when(jnp.logical_not(is_image))
    def _():
        pltpu.make_async_copy(text_feats, feats.at[own], local_sem.at[0]).start()
        pltpu.make_async_copy(text_proj, proj, local_sem.at[1]).start()

    barrier = pltpu.get_barrier_semaphore()
    partners = [along(axis, step) for axis in range(3) for step in (1, 2, 3)] + [sibling]
    for partner in partners:
        pl.semaphore_signal(barrier, inc=1, device_id=partner, device_id_type=MESH)
    pl.semaphore_wait(barrier, len(partners))

    def cross(src):
        return remote(src, feats.at[own], gather_send.at[14], gather_recv.at[1], sibling)

    @pl.when(is_image)
    def _():
        cross(text_feats).start()

    @pl.when(jnp.logical_not(is_image))
    def _():
        cross(image_feats).start()

    own_copy.wait()

    sends = {}
    for index, (path, to) in enumerate(((RING_UP, ring(1)), (RING_DOWN, ring(3)), (ACROSS, across))):
        for step, (source, target) in enumerate(path):
            sends[(index, step)] = remote(
                feats.at[slot(source)], feats.at[slot(target)], gather_send.at[index * 5 + step], arrival(target), to
            )

    def arrived(*key):
        remote(feats.at[slot(key)], feats.at[slot(key)], gather_send.at[0], arrival(key), sibling).wait_recv()

    for index in range(3):
        sends[(index, 0)].start()
    arrived(0, 0, 1)
    for index in range(3):
        sends[(index, 1)].start()
    proj_copy.wait()

    def unit_copy(index):
        rows = pl.ds(pl.multiple_of(index * UNIT, UNIT), UNIT)
        return remote(unit.at[rows], other.at[rows], unit_send.at[index], unit_recv.at[index], sibling)

    def project(index, buffer):
        rows = pl.ds(pl.multiple_of(index * UNIT, UNIT), UNIT)
        buffer[pl.ds(0, UNIT), :] = jnp.dot(feats[rows, :], proj[...], preferred_element_type=F32)
        feats_t[:, rows] = feats[rows, :].T

    def normalize(index, buffer):
        for i in range(UNIT // STEP):
            there = pl.ds(pl.multiple_of(index * UNIT + i * STEP, STEP), STEP)
            raw = buffer[pl.ds(i * STEP, STEP), :]
            inv = 1.0 / jnp.sqrt(jnp.sum(raw * raw, axis=1, keepdims=True) + 1e-06)
            value = raw * inv
            half = value.astype(BF16)
            unit[there, :] = half
            unit_low[there, :] = (value - half.astype(F32)).astype(BF16)
            inv_norm[there, :] = inv

    def three_units(first):
        project(first, wide)
        project(first + 1, perm)
        normalize(first, wide)
        unit_copy(first).start()
        project(first + 2, wide)
        normalize(first + 1, perm)
        unit_copy(first + 1).start()
        normalize(first + 2, wide)
        unit_copy(first + 2).start()

    scale = jnp.exp(jnp.full((1, TILE), log_scale[0], F32))
    slope = scale * LOG2E
    offset = jnp.full((1, TILE), logit_bias[0], F32) * LOG2E

    def tile_copy(t, a, b):
        return remote(
            pairs_t.at[t],
            pairs.at[pl.ds(pl.multiple_of(b * TILE, TILE), TILE), pl.ds(pl.multiple_of(a * TILE, TILE), TILE)],
            tile_send.at[t], tile_recv.at[t], sibling,
        )

    def tile_place(t):
        a = jnp.where(t < 4, lax.rem(t, 2), 2 + lax.div(t - 4, 2))
        b = lax.rem(a + core, 2) + jnp.where(t < 2, 0, jnp.where(t < 4, 2, 2 * lax.rem(t, 2)))
        return a, b

    def cosines(t, buffer):
        a, b = tile_place(t)
        rows = pl.ds(pl.multiple_of(a * TILE, TILE), TILE)
        cols = pl.ds(pl.multiple_of(b * TILE, TILE), TILE)
        buffer[pl.ds(0, TILE), pl.ds(0, TILE)] = lax.dot_general(
            unit[rows, :], other[cols, :], (((1,), (1,)), ((), ())), preferred_element_type=F32
        )

    def pair_terms(t, buffer, diagonal):
        a, b = tile_place(t)
        cols = pl.ds(pl.multiple_of(b * TILE, TILE), TILE)
        acc = [jnp.zeros((8, TILE), F32) for _ in range(3)]
        for i in range(TILE // STEP):
            cosine = buffer[pl.ds(i * STEP, STEP), pl.ds(0, TILE)]
            arg = cosine * slope + offset
            masked = diagonal and i < UNIT // STEP
            if masked:
                row = i * STEP + lax.broadcasted_iota(jnp.int32, (STEP, TILE), 0)
                col = lax.broadcasted_iota(jnp.int32, (STEP, TILE), 1) + core * ROWS
                sign = jnp.where(row == col, -1.0, 1.0).astype(F32)
                arg = arg * sign
            up = jnp.exp2(arg)
            whole = 1.0 + up
            inv = pl.reciprocal(whole, approx=True)
            inv = inv * (2.0 - whole * inv)
            grad = up * inv
            loss = jnp.log(whole) + (up - (whole - 1.0)) * inv
            if masked:
                grad = grad * sign
            pairs[pl.ds(pl.multiple_of(a * TILE + i * STEP, STEP), STEP), cols] = grad.astype(BF16)
            acc = [acc[0] + fold(loss), acc[1] + fold(grad * cosine), acc[2] + fold(grad)]
        for k in range(3):
            sums[k] += acc[k]

    def hand_over(t):
        a, b = tile_place(t)
        rows = pl.ds(pl.multiple_of(a * TILE, TILE), TILE)
        cols = pl.ds(pl.multiple_of(b * TILE, TILE), TILE)
        pairs_t[t] = pairs[rows, cols].T
        tile_copy(t, a, b).start()

    def two_tiles(i, carry):
        t = 2 * i
        cosines(t + 1, perm)
        pair_terms(t, wide, False)
        hand_over(t)
        cosines(t + 2, wide)
        pair_terms(t + 1, perm, False)
        hand_over(t + 1)
        return carry

    sums[...] = jnp.zeros_like(sums)
    project(0, wide)
    normalize(0, wide)
    unit_copy(0).start()
    arrived(0, 1, 0)
    sends[(1, 2)].start()
    sends[(2, 2)].start()
    arrived(0, 3, 0)
    sends[(2, 3)].start()
    arrived(1, 0, 0)
    arrived(1, 0, 1)
    sends[(0, 2)].start()
    sends[(1, 3)].start()
    arrived(0, 3, 1)
    sends[(0, 3)].start()
    arrived(0, 1, 1)
    three_units(1)
    arrived(1, 3, 1)
    sends[(0, 4)].start()
    arrived(1, 1, 0)
    sends[(1, 4)].start()
    for index in range(4):
        unit_copy(index).wait_recv()
    cosines(0, wide)
    cosines(1, perm)
    pair_terms(0, wide, True)
    hand_over(0)
    pair_terms(1, perm, False)
    hand_over(1)
    for key in ((0, 2, 0), (0, 2, 1), (1, 1, 1), (1, 3, 0)):
        arrived(*key)
    three_units(4)
    arrived(1, 2, 0)
    arrived(1, 2, 1)
    project(7, wide)
    normalize(7, wide)
    unit_copy(7).start()
    for index in range(4, 8):
        unit_copy(index).wait_recv()
    cosines(2, wide)
    lax.fori_loop(1, 3, two_tiles, 0)
    cosines(7, perm)
    pair_terms(6, wide, False)
    hand_over(6)
    pair_terms(7, perm, False)
    hand_over(7)

    def scalar_copies(stage):
        if stage == 3:
            return [remote(scalars.at[3, core], scalars.at[3, core], scalar_send.at[9], scalar_recv.at[9], sibling)]
        return [
            remote(
                scalars.at[stage, pos[stage]], scalars.at[stage, pos[stage]],
                scalar_send.at[stage * 3 + step - 1], scalar_recv.at[stage * 3 + step - 1], along(stage, step),
            )
            for step in (1, 2, 3)
        ]

    def scalar_start(stage, value):
        scalars[stage, pos[stage] if stage < 3 else core] = value
        for copy in scalar_copies(stage):
            copy.start()

    def scalar_finish(stage):
        for copy in scalar_copies(stage):
            copy.wait()
        if stage == 3:
            return scalars[3, 0] + scalars[3, 1]
        return (scalars[stage, 0] + scalars[stage, 1]) + (scalars[stage, 2] + scalars[stage, 3])

    lanes = [sums[k][:, 0:128] + sums[k][:, 128:256] + (sums[k][:, 256:384] + sums[k][:, 384:512]) for k in range(3)]
    scalar_start(0, jnp.concatenate(lanes, axis=0))

    for copy in sends.values():
        copy.wait_send()
    cross(text_feats).wait_send()
    for t in range(8):
        tile_copy(t, 0, 0).wait_recv()

    scale_row = jnp.exp(jnp.full((1, 1), log_scale[0], F32))

    def gradients(a, buffer):
        buffer[pl.ds(0, TILE), :] = jnp.dot(pairs[pl.ds(a * TILE, TILE), :], other[...], preferred_element_type=F32)

    def tangents(a, buffer):
        for i in range(TILE // STEP):
            there = pl.ds(a * TILE + i * STEP, STEP)
            grad = buffer[pl.ds(i * STEP, STEP), :]
            value = unit[there, :].astype(F32) + unit_low[there, :].astype(F32)
            inner = jnp.sum(value * grad, axis=1, keepdims=True)
            feats[there, :] = ((grad - value * inner) * (inv_norm[there, :] * scale_row)).astype(BF16)

    gradients(0, wide)
    for a in range(1, 4):
        gradients(a, (wide, perm)[a % 2])
        tangents(a - 1, (perm, wide)[a % 2])
    tangents(3, perm)
    scalar_start(1, scalar_finish(0))

    def weights(t):
        cols = pl.ds(pl.multiple_of(t * THIRD, PART), THIRD)
        wide[:, cols] = jnp.dot(feats_t[...], feats[:, cols], preferred_element_type=F32)

    up = 1 - 2 * core

    def columns(t, p):
        return pl.ds(pl.multiple_of(t * THIRD + p * PART, PART), PART)

    def first_copies(t, p):
        axis, q = ORDERS[p][0], t * 3 + p
        ahead, behind = along(axis, lax.rem(4 + up, 4)), along(axis, lax.rem(4 - up, 4))
        return (
            remote(first_a.at[q], into_a.at[q], first_send.at[q, 0], first_recv.at[q, 0], ahead),
            remote(first_b.at[q], into_b.at[q], first_send.at[q, 1], first_recv.at[q, 1], behind),
            remote(into_a.at[q], into_c.at[q], first_send.at[q, 2], first_recv.at[q, 2], ahead),
        )

    def block(t, p, step):
        k = lax.rem(pos[ORDERS[p][0]] + 4 + step, 4)
        return pl.ds(pl.multiple_of(k * 288, 288), 288), columns(t, p)

    def first_start(t, p):
        for k1 in range(4):
            for k2 in range(4):
                for k3 in range(4):
                    place = [0, 0, 0]
                    for axis, k in zip(ORDERS[p], (k1, k2, k3)):
                        place[axis] = k
                    perm[pl.ds(k1 * 288 + k2 * 72 + k3 * 18, 18), columns(t, p)] = (
                        wide[pl.ds(natural_row(*place), 18), columns(t, p)])
        q = t * 3 + p
        first_a[q] = perm[block(t, p, 2)].astype(BF16)
        first_b[q] = perm[block(t, p, -up)].astype(BF16)
        copies = first_copies(t, p)
        copies[0].start()
        copies[1].start()

    def first_forward(t, p):
        copies, q = first_copies(t, p), t * 3 + p
        copies[0].wait_recv()
        into_a[q] = (perm[block(t, p, up)] + into_a[q].astype(F32)).astype(BF16)
        copies[2].start()

    def second_copies(t, p):
        q = t * 3 + p
        return [
            remote(second_out.at[q, step - 1], second_in.at[q, step - 1], second_send.at[q, step - 1],
                   second_recv.at[q, step - 1], along(ORDERS[p][1], step))
            for step in (1, 2, 3)
        ]

    def second_rows(p, step):
        return pl.ds(pl.multiple_of(lax.rem(pos[ORDERS[p][1]] + step, 4) * 72, 8), 72)

    def second_start(t, p):
        copies, q = first_copies(t, p), t * 3 + p
        copies[1].wait_recv()
        copies[2].wait_recv()
        part_sum[q] = perm[block(t, p, 0)] + into_b[q].astype(F32) + into_c[q].astype(F32)
        for step, copy in zip((1, 2, 3), second_copies(t, p)):
            second_out[q, step - 1, pl.ds(0, 72), :] = part_sum[q, second_rows(p, step), :].astype(BF16)
            copy.start()

    def third_copies(t, p):
        at, q = pos[ORDERS[p][2]], t * 3 + p
        return [
            remote(third_own.at[q, lax.rem(at + step, 4)], third_in.at[q, step - 1], third_send.at[q, step - 1],
                   third_recv.at[q, step - 1], along(ORDERS[p][2], step))
            for step in (1, 2, 3)
        ]

    def third_start(t, p):
        q = t * 3 + p
        total = part_sum[q, second_rows(p, 0), :]
        for step, copy in zip((1, 2, 3), second_copies(t, p)):
            copy.wait_recv()
            total += second_in[q, step - 1, pl.ds(0, 72), :].astype(F32)
        part_sum[q, pl.ds(0, 72), :] = total
        for k in range(4):
            third_own[q, k, pl.ds(0, 18), :] = part_sum[q, pl.ds(18 * k, 18), :]
        for copy in third_copies(t, p):
            copy.start()

    def third_finish(t, p):
        q = t * 3 + p
        total = third_own[q, pos[ORDERS[p][2]], pl.ds(0, 18), :]
        for step, copy in zip((1, 2, 3), third_copies(t, p)):
            copy.wait_recv()
            total += third_in[q, step - 1, pl.ds(0, 18), :]
        part_sum[q, pl.ds(0, 18), :] = total
        for h in range(2):
            last[h, pl.ds(0, 9), columns(t, p)] = part_sum[q, pl.ds(9 * h, 9), :]

    def each(step, t):
        for p in range(3):
            step(t, p)

    def third(t, carry):
        weights(t)

        @pl.when(t > 0)
        def _():
            each(first_forward, t - 1)

        each(first_start, t)

        @pl.when(t > 1)
        def _():
            each(second_start, t - 2)

        return carry

    lax.fori_loop(0, 3, third, 0)
    scalar_start(2, scalar_finish(1))
    each(first_forward, 2)
    each(second_start, 1)
    each(third_start, 0)
    each(second_start, 2)
    scalar_start(3, scalar_finish(2))
    each(third_start, 1)
    each(third_finish, 0)
    each(third_start, 2)
    each(third_finish, 1)
    totals = scalar_finish(3)
    batch = 1.0 / 16384.0
    loss_out[0] = jnp.sum(totals[0:8]) * batch
    scale_out[0] = jnp.sum(totals[8:16] * jnp.exp(jnp.full((8, 128), log_scale[0], F32))) * batch
    bias_out[0] = jnp.sum(totals[16:24]) * batch
    each(third_finish, 2)

    exchange = remote(last.at[1 - core], last_in, last_sem.at[0], last_sem.at[1], sibling)
    exchange.start()

    def sent(t, carry):
        for p in range(3):
            for copy in first_copies(t, p) + tuple(second_copies(t, p)) + tuple(third_copies(t, p)):
                copy.wait_send()
        return carry

    lax.fori_loop(0, 3, sent, 0)
    for index in range(8):
        unit_copy(index).wait_send()
        tile_copy(index, 0, 0).wait_send()
    exchange.wait()
    rows = pl.ds(0, 9)

    @pl.when(is_image)
    def _():
        image_out[...] = last[0, rows, :]
        text_out[...] = last_in[rows, :]

    @pl.when(jnp.logical_not(is_image))
    def _():
        image_out[...] = last_in[rows, :]
        text_out[...] = last[1, rows, :]


def per_device(image_feats, text_feats, image_proj, text_proj, log_scale, logit_bias):
    smem = pl.BlockSpec(memory_space=pltpu.SMEM)
    vmem = pl.BlockSpec(memory_space=pltpu.VMEM)
    hbm = pl.BlockSpec(memory_space=pl.ANY)
    dma, buffer = pltpu.SemaphoreType.DMA, pltpu.VMEM
    one = jax.ShapeDtypeStruct((1,), F32)
    rows = jax.ShapeDtypeStruct((9, WIDTH), F32)
    loss, image_grad, text_grad, scale_grad, bias_grad = pl.pallas_call(
        kernel,
        out_shape=(one, rows, rows, one, one),
        in_specs=[smem, smem, hbm, hbm, hbm, hbm],
        out_specs=(smem, vmem, vmem, smem, smem),
        scratch_shapes=[
            buffer((ROWS, WIDTH), BF16),
            buffer((WIDTH, ROWS), BF16),
            buffer((ROWS, WIDTH), BF16),
            buffer((ROWS, WIDTH), BF16),
            buffer((ROWS, WIDTH), BF16),
            buffer((ROWS, ROWS), BF16),
            buffer((8, TILE, TILE), BF16),
            buffer((WIDTH, WIDTH), BF16),
            buffer((ROWS, 1), F32),
            buffer((WIDTH, WIDTH), F32),
            buffer((WIDTH, WIDTH), F32),
            buffer((3, 8, TILE), F32),
            *[buffer((9, 288, PART), BF16) for _ in range(5)],
            buffer((9, 288, PART), F32),
            buffer((9, 3, 80, PART), BF16),
            buffer((9, 3, 80, PART), BF16),
            buffer((9, 4, 24, PART), F32),
            buffer((9, 3, 24, PART), F32),
            buffer((4, 4, 24, 128), F32),
            buffer((2, 16, WIDTH), F32),
            buffer((16, WIDTH), F32),
            dma((2,)),
            dma((15,)), dma((16,)),
            dma((8,)), dma((8,)),
            dma((8,)), dma((8,)),
            *[dma((9, 3)) for _ in range(6)],
            dma((10,)), dma((10,)),
            dma((2,)),
        ],
        compiler_params=pltpu.CompilerParams(collective_id=0, has_side_effects=True, vmem_limit_bytes=63 * 2**20),
        name="sigmoid_loss",
    )(log_scale, logit_bias, image_feats, text_feats, image_proj, text_proj)
    return loss, image_grad, text_grad, scale_grad, bias_grad


def solution(mesh):
    return jax.shard_map(
        per_device,
        mesh=mesh,
        in_specs=(P(("dp", "mp"), None), P(("dp", "mp"), None), P(), P(), P(), P()),
        out_specs=(P(), P(("dp", "mp"), None), P(("dp", "mp"), None), P(), P()),
        check_vma=False,
    )
```

time: 120 us -> 99.7 us (0.83)
  Pallas kernels: 109 us -> 89.2 us
    pallas_call x1, Pallas kernels: 109 us -> 89.2 us  [per_device(): pl.pallas_call(kernel, out_shape=(one, rows, rows, one, one), in_specs=[s...]
where the time goes in v2:
time: 99.7 us; the launch traced here: 99.4 us
  Pallas kernels  89.2 us (89%)
  between operations  7.21 us (7%)
  local copies, waits for them, and re-layouts  3.04 us (3%)
    pallas_call x1, Pallas kernels, per_device(): pl.pallas_call(kernel, out_shape=(one, rows, rows, one, one), in_specs=[s...  89.2 us
    unnamed x2, local copies, waits for them, and re-layouts  3.04 us

profile of v2, /device:TPU:1, one launch (start us, length us, event | category | flops | bytes accessed | tf_op | source)
XLA Modules:
  0.0 99.4 jit_solution(10342807482858040839)
XLA Ops:
  1.9 89.2 %sigmoid_loss.1 = (f32[1]{0:T(128)}, f32[9,1152]{1,0:T(8,128)}, f32[9,1152]{1,0:T(8,128)}, f32[1]{0:T(128)}, f32[1]{0:T(128)}) custom-call(f32[1]{0:T(128)S(6)} %copy.16.log_scale, f32[1]{0:T(128)S(6)} %copy.17.logit_bias, bf16[128,1152]{1,0:T(8,128)(2,1)} %image_feats.1, bf16[128,1152]{1,0:T(8,128)(2,1)} %text_feats.1, bf16[1152,1152]{1,0:T(8,128)(2,1)} %image_proj.1, ...), custom_call_target="tpu_custom_call" | custom-call | tf_op jit(solution)/shard_map/sigmoid_loss/pallas_call | solution.py:496
  91.7 1.5 %copy.19 = f32[9,1152]{1,0:T(8,128)} copy(f32[9,1152]{1,0:T(8,128)} %get-tuple-element.11) | data formatting | bytes 82944
  93.2 1.5 %copy.20 = f32[9,1152]{1,0:T(8,128)} copy(f32[9,1152]{1,0:T(8,128)} %get-tuple-element.12) | data formatting | bytes 82944

commit v3 on v2

--- a/solution.py
+++ b/solution.py
@@ -23,6 +23,10 @@
 RING_UP = [((0, 0, 0), (0, 3, 0)), ((0, 0, 1), (0, 3, 1)), ((1, 0, 1), (1, 3, 1)), ((0, 3, 1), (0, 2, 1)), ((1, 3, 1), (1, 2, 1))]
 RING_DOWN = [((0, 0, 0), (0, 1, 0)), ((0, 0, 1), (0, 1, 1)), ((0, 1, 0), (0, 2, 0)), ((1, 0, 1), (1, 1, 1)), ((1, 1, 0), (1, 2, 0))]
 ACROSS = [((0, 0, 0), (1, 0, 0)), ((0, 0, 1), (1, 0, 1)), ((0, 1, 0), (1, 1, 0)), ((0, 3, 0), (1, 3, 0))]
+TILES = [
+    [(0, 0), (1, 1), (0, 2), (2, 0), (2, 2), (1, 3), (3, 1), (3, 3)],
+    [(0, 1), (1, 0), (1, 2), (2, 1), (0, 3), (2, 3), (3, 0), (3, 2)],
+]
 ORDERS = [(0, 1, 2), (1, 2, 0), (2, 0, 1)]
 
 
@@ -41,12 +45,12 @@
 
 def kernel(
     log_scale, logit_bias, image_feats, text_feats, image_proj, text_proj,
-    loss_out, image_out, text_out, scale_out, bias_out,
+    out,
     feats, feats_t, unit, unit_low, other, pairs, pairs_t, proj, inv_norm, wide, perm, sums,
     first_a, first_b, into_a, into_b, into_c, part_sum, second_out, second_in, third_own, third_in,
-    scalars, last, last_in,
+    scalars,
     local_sem, gather_send, gather_recv, unit_send, unit_recv, tile_send, tile_recv,
-    first_send, first_recv, second_send, second_recv, third_send, third_recv, scalar_send, scalar_recv, last_sem,
+    first_send, first_recv, second_send, second_recv, third_send, third_recv, scalar_send, scalar_recv,
 ):
     dp, mp = lax.axis_index("dp"), lax.axis_index("mp")
     core = lax.rem(mp, 2)
@@ -57,10 +61,10 @@
     is_image = core == 0
     sibling = (dp, mp + 1 - 2 * core)
 
-    def along(axis, step):
+    def along(axis, step, other_core=False):
         moved = [x, y, z]
         moved[axis] = moved[axis] + step
-        return device(*moved, core)
+        return device(*moved, 1 - core if other_core else core)
 
     def ring(step):
         return device(jnp.where(is_image, x, x + step), y, jnp.where(is_image, z + step, z), core)
@@ -96,7 +100,7 @@
         pltpu.make_async_copy(text_proj, proj, local_sem.at[1]).start()
 
     barrier = pltpu.get_barrier_semaphore()
-    partners = [along(axis, step) for axis in range(3) for step in (1, 2, 3)] + [sibling]
+    partners = [along(axis, step, flip) for axis in range(3) for step in (1, 2, 3) for flip in (False, True)] + [sibling]
     for partner in partners:
         pl.semaphore_signal(barrier, inc=1, device_id=partner, device_id_type=MESH)
     pl.semaphore_wait(barrier, len(partners))
@@ -174,9 +178,13 @@
         )
 
     def tile_place(t):
-        a = jnp.where(t < 4, lax.rem(t, 2), 2 + lax.div(t - 4, 2))
-        b = lax.rem(a + core, 2) + jnp.where(t < 2, 0, jnp.where(t < 4, 2, 2 * lax.rem(t, 2)))
-        return a, b
+        place = []
+        for k in range(2):
+            found = [jnp.int32(TILES[c][7][k]) for c in range(2)]
+            for i in range(7):
+                found = [jnp.where(t == i, TILES[c][i][k], found[c]) for c in range(2)]
+            place.append(jnp.where(is_image, found[0], found[1]))
+        return place
 
     def cosines(t, buffer):
         a, b = tile_place(t)
@@ -224,6 +232,12 @@
         cosines(t + 1, perm)
         pair_terms(t, wide, False)
         hand_over(t)
+
+        @pl.when(i == 1)
+        def _():
+            for index in range(6, 8):
+                unit_copy(index).wait_recv()
+
         cosines(t + 2, wide)
         pair_terms(t + 1, perm, False)
         hand_over(t + 1)
@@ -266,7 +280,7 @@
     project(7, wide)
     normalize(7, wide)
     unit_copy(7).start()
-    for index in range(4, 8):
+    for index in range(4, 6):
         unit_copy(index).wait_recv()
     cosines(2, wide)
     lax.fori_loop(1, 3, two_tiles, 0)
@@ -305,27 +319,34 @@
     for copy in sends.values():
         copy.wait_send()
     cross(text_feats).wait_send()
-    for t in range(8):
+    for t in range(6):
         tile_copy(t, 0, 0).wait_recv()
 
     scale_row = jnp.exp(jnp.full((1, 1), log_scale[0], F32))
 
     def gradients(a, buffer):
-        buffer[pl.ds(0, TILE), :] = jnp.dot(pairs[pl.ds(a * TILE, TILE), :], other[...], preferred_element_type=F32)
+        rows = pl.ds(pl.multiple_of(a * TILE, TILE), TILE)
+        buffer[pl.ds(0, TILE), :] = jnp.dot(pairs[rows, :], other[...], preferred_element_type=F32)
 
     def tangents(a, buffer):
         for i in range(TILE // STEP):
-            there = pl.ds(a * TILE + i * STEP, STEP)
+            there = pl.ds(pl.multiple_of(a * TILE + i * STEP, STEP), STEP)
             grad = buffer[pl.ds(i * STEP, STEP), :]
             value = unit[there, :].astype(F32) + unit_low[there, :].astype(F32)
             inner = jnp.sum(value * grad, axis=1, keepdims=True)
             feats[there, :] = ((grad - value * inner) * (inv_norm[there, :] * scale_row)).astype(BF16)
 
-    gradients(0, wide)
-    for a in range(1, 4):
-        gradients(a, (wide, perm)[a % 2])
-        tangents(a - 1, (perm, wide)[a % 2])
-    tangents(3, perm)
+    order = (1 - core, 3 - core, core, 2 + core)
+    gradients(order[0], wide)
+    gradients(order[1], perm)
+    tangents(order[0], wide)
+    for t in range(6, 8):
+        tile_copy(t, 0, 0).wait_recv()
+    gradients(order[2], wide)
+    tangents(order[1], perm)
+    gradients(order[3], perm)
+    tangents(order[2], wide)
+    tangents(order[3], perm)
     scalar_start(1, scalar_finish(0))
 
     def weights(t):
@@ -393,12 +414,17 @@
             copy.start()
 
     def third_copies(t, p):
-        at, q = pos[ORDERS[p][2]], t * 3 + p
-        return [
-            remote(third_own.at[q, lax.rem(at + step, 4)], third_in.at[q, step - 1], third_send.at[q, step - 1],
-                   third_recv.at[q, step - 1], along(ORDERS[p][2], step))
-            for step in (1, 2, 3)
-        ]
+        axis, q = ORDERS[p][2], t * 3 + p
+        copies = []
+        for flip in (False, True):
+            half = 1 - core if flip else core
+            for step in range(4):
+                if step or flip:
+                    sem = 3 + step if flip else step - 1
+                    copies.append(remote(
+                        third_own.at[q, lax.rem(pos[axis] + step, 4), half], third_in.at[q, core, step],
+                        third_send.at[q, sem], third_recv.at[q, sem], along(axis, step, flip)))
+        return copies
 
     def third_start(t, p):
         q = t * 3 + p
@@ -408,19 +434,19 @@
             total += second_in[q, step - 1, pl.ds(0, 72), :].astype(F32)
         part_sum[q, pl.ds(0, 72), :] = total
         for k in range(4):
-            third_own[q, k, pl.ds(0, 18), :] = part_sum[q, pl.ds(18 * k, 18), :]
+            for h in range(2):
+                third_own[q, k, h, pl.ds(0, 9), :] = part_sum[q, pl.ds(18 * k + 9 * h, 9), :]
         for copy in third_copies(t, p):
             copy.start()
+        third_in[q, core, 0] = third_own[q, pos[ORDERS[p][2]], core]
 
     def third_finish(t, p):
         q = t * 3 + p
-        total = third_own[q, pos[ORDERS[p][2]], pl.ds(0, 18), :]
-        for step, copy in zip((1, 2, 3), third_copies(t, p)):
+        for copy in third_copies(t, p):
             copy.wait_recv()
-            total += third_in[q, step - 1, pl.ds(0, 18), :]
-        part_sum[q, pl.ds(0, 18), :] = total
-        for h in range(2):
-            last[h, pl.ds(0, 9), columns(t, p)] = part_sum[q, pl.ds(9 * h, 9), :]
+        for side in range(2):
+            got = [third_in[q, side, step, pl.ds(0, 9), :] for step in range(4)]
+            out[pl.ds(16 * side, 9), columns(t, p)] = (got[0] + got[1]) + (got[2] + got[3])
 
     def each(step, t):
         for p in range(3):
@@ -454,13 +480,10 @@
     each(third_finish, 1)
     totals = scalar_finish(3)
     batch = 1.0 / 16384.0
-    loss_out[0] = jnp.sum(totals[0:8]) * batch
-    scale_out[0] = jnp.sum(totals[8:16] * jnp.exp(jnp.full((8, 128), log_scale[0], F32))) * batch
-    bias_out[0] = jnp.sum(totals[16:24]) * batch
+    row_scale = jnp.exp(jnp.full((8, 128), log_scale[0], F32))
+    for k, value in enumerate((totals[0:8], totals[8:16] * row_scale, totals[16:24])):
+        out[pl.ds(9 + k, 1), pl.ds(0, 128)] = jnp.full((1, 128), jnp.sum(value) * batch, F32)
     each(third_finish, 2)
-
-    exchange = remote(last.at[1 - core], last_in, last_sem.at[0], last_sem.at[1], sibling)
-    exchange.start()
 
     def sent(t, carry):
         for p in range(3):
@@ -472,18 +495,13 @@
     for index in range(8):
         unit_copy(index).wait_send()
         tile_copy(index, 0, 0).wait_send()
-    exchange.wait()
-    rows = pl.ds(0, 9)
-
-    @pl.when(is_image)
-    def _():
-        image_out[...] = last[0, rows, :]
-        text_out[...] = last_in[rows, :]
-
-    @pl.when(jnp.logical_not(is_image))
-    def _():
-        image_out[...] = last_in[rows, :]
-        text_out[...] = last[1, rows, :]
+
+def split(packed, loss_out, image_out, text_out, scale_out, bias_out):
+    image_out[...] = packed[pl.ds(0, 9), :]
+    text_out[...] = packed[pl.ds(16, 9), :]
+    loss_out[0] = packed[9, 0]
+    scale_out[0] = packed[10, 0]
+    bias_out[0] = packed[11, 0]
 
 
 def per_device(image_feats, text_feats, image_proj, text_proj, log_scale, logit_bias):
@@ -493,11 +511,11 @@
     dma, buffer = pltpu.SemaphoreType.DMA, pltpu.VMEM
     one = jax.ShapeDtypeStruct((1,), F32)
     rows = jax.ShapeDtypeStruct((9, WIDTH), F32)
-    loss, image_grad, text_grad, scale_grad, bias_grad = pl.pallas_call(
+    packed = pl.pallas_call(
         kernel,
-        out_shape=(one, rows, rows, one, one),
+        out_shape=jax.ShapeDtypeStruct((32, WIDTH), F32),
         in_specs=[smem, smem, hbm, hbm, hbm, hbm],
-        out_specs=(smem, vmem, vmem, smem, smem),
+        out_specs=vmem,
         scratch_shapes=[
             buffer((ROWS, WIDTH), BF16),
             buffer((WIDTH, ROWS), BF16),
@@ -515,23 +533,27 @@
             buffer((9, 288, PART), F32),
             buffer((9, 3, 80, PART), BF16),
             buffer((9, 3, 80, PART), BF16),
-            buffer((9, 4, 24, PART), F32),
-            buffer((9, 3, 24, PART), F32),
+            buffer((9, 4, 2, 16, PART), F32),
+            buffer((9, 2, 4, 16, PART), F32),
             buffer((4, 4, 24, 128), F32),
-            buffer((2, 16, WIDTH), F32),
-            buffer((16, WIDTH), F32),
             dma((2,)),
             dma((15,)), dma((16,)),
             dma((8,)), dma((8,)),
             dma((8,)), dma((8,)),
-            *[dma((9, 3)) for _ in range(6)],
+            *[dma((9, 3)) for _ in range(4)],
+            dma((9, 7)), dma((9, 7)),
             dma((10,)), dma((10,)),
-            dma((2,)),
         ],
         compiler_params=pltpu.CompilerParams(collective_id=0, has_side_effects=True, vmem_limit_bytes=63 * 2**20),
         name="sigmoid_loss",
     )(log_scale, logit_bias, image_feats, text_feats, image_proj, text_proj)
-    return loss, image_grad, text_grad, scale_grad, bias_grad
+    return pl.pallas_call(
+        split,
+        out_shape=(one, rows, rows, one, one),
+        in_specs=[vmem],
+        out_specs=(smem, vmem, vmem, smem, smem),
+        name="split_outputs",
+    )(packed)
 
 
 def solution(mesh):

time: 99.7 us -> 89.3 us (0.90)
  between operations: 7.21 us -> 2.11 us
  local copies, waits for them, and re-layouts: 3.04 us -> 0 us
  Pallas kernels: 89.2 us -> 87 us
    unnamed x2 -> x0, local copies, waits for them, and re-layouts: 3.04 us -> none
    pallas_call x1 -> x2, Pallas kernels: 89.2 us -> 87 us  [the longest x1 85.4 us: per_device(): pl.pallas_call(kernel, out_shape=jax.ShapeDtypeStruct((32, WIDTH), F32),...]
where the time goes in v3:
time: 89.3 us; the launch traced here: 89.1 us
  Pallas kernels  87 us (97%)
  between operations  2.11 us (2%)
    pallas_call x1, Pallas kernels, per_device(): pl.pallas_call(kernel, out_shape=jax.ShapeDtypeStruct((32, WIDTH), F32),...  85.4 us

profile of v3, /device:TPU:1, one launch (start us, length us, event | category | flops | bytes accessed | tf_op | source)
XLA Modules:
  0.0 89.1 jit_solution(2603791885969069504)
XLA Ops:
  1.9 85.4 %sigmoid_loss.1.packed = f32[32,1152]{1,0:T(8,128)} custom-call(f32[1]{0:T(128)S(6)} %copy.11.log_scale, f32[1]{0:T(128)S(6)} %copy.12.logit_bias, bf16[128,1152]{1,0:T(8,128)(2,1)} %image_feats.1, bf16[128,1152]{1,0:T(8,128)(2,1)} %text_feats.1, bf16[1152,1152]{1,0:T(8,128)(2,1)} %image_proj.1, bf16[1152,1152]{1,0:T(8,128)(2,1)} %text_proj.1), custom_call_target="tpu_custom_call" | custom-call | tf_op jit(solution)/shard_map/sigmoid_loss/pallas_call | solution.py:514
  87.4 1.6 %split_outputs.1 = (f32[1]{0:T(128)}, f32[9,1152]{1,0:T(8,128)}, f32[9,1152]{1,0:T(8,128)}, f32[1]{0:T(128)}, f32[1]{0:T(128)}) custom-call(f32[32,1152]{1,0:T(8,128)} %sigmoid_loss.1.packed), custom_call_target="tpu_custom_call" | custom-call | tf_op jit(solution)/shard_map/split_outputs/pallas_call | solution.py:550

commit v4 on v3

--- a/solution.py
+++ b/solution.py
@@ -15,19 +15,22 @@
 ROWS = 8 * UNIT
 TILE = 512
 PART = 128
-THIRD = 3 * PART
 STEP = 16
 LOG2E = 1.4426950408889634
 
 UNITS = {(0, 0): 0, (1, 0): 1, (0, 3): 2, (0, 1): 3, (1, 3): 4, (1, 1): 5, (0, 2): 6, (1, 2): 7}
-RING_UP = [((0, 0, 0), (0, 3, 0)), ((0, 0, 1), (0, 3, 1)), ((1, 0, 1), (1, 3, 1)), ((0, 3, 1), (0, 2, 1)), ((1, 3, 1), (1, 2, 1))]
-RING_DOWN = [((0, 0, 0), (0, 1, 0)), ((0, 0, 1), (0, 1, 1)), ((0, 1, 0), (0, 2, 0)), ((1, 0, 1), (1, 1, 1)), ((1, 1, 0), (1, 2, 0))]
-ACROSS = [((0, 0, 0), (1, 0, 0)), ((0, 0, 1), (1, 0, 1)), ((0, 1, 0), (1, 1, 0)), ((0, 3, 0), (1, 3, 0))]
+RING_UP = [((0, 0, 0), (0, 3, 0)), ((0, 0, 1), (0, 3, 1)), ((0, 3, 0), (0, 2, 0)), ((1, 0, 1), (1, 3, 1)), ((1, 3, 0), (1, 2, 0))]
+RING_DOWN = [((0, 0, 0), (0, 1, 0)), ((0, 0, 1), (0, 1, 1)), ((1, 0, 1), (1, 1, 1)), ((0, 1, 1), (0, 2, 1)), ((1, 1, 1), (1, 2, 1))]
+ACROSS = [((0, 0, 1), (1, 0, 1)), ((0, 0, 0), (1, 0, 0)), ((0, 3, 0), (1, 3, 0)), ((0, 1, 0), (1, 1, 0))]
 TILES = [
     [(0, 0), (1, 1), (0, 2), (2, 0), (2, 2), (1, 3), (3, 1), (3, 3)],
     [(0, 1), (1, 0), (1, 2), (2, 1), (0, 3), (2, 3), (3, 0), (3, 2)],
 ]
 ORDERS = [(0, 1, 2), (1, 2, 0), (2, 0, 1)]
+
+BATCHES = [(0, 3, 6), (1, 4), (2, 5), (7,), (8,)]
+SECOND = [(0, 240), (240, 160), (400, 160), (560, 80), (640, 80)]
+THIRD = [(0, 32), (32, 24), (56, 24), (80, 16), (96, 16)]
 
 
 def device(x, y, z, core):
@@ -100,7 +103,8 @@
         pltpu.make_async_copy(text_proj, proj, local_sem.at[1]).start()
 
     barrier = pltpu.get_barrier_semaphore()
-    partners = [along(axis, step, flip) for axis in range(3) for step in (1, 2, 3) for flip in (False, True)] + [sibling]
+    known = {(axis, step, flip): along(axis, step, flip) for axis in range(3) for step in (1, 2, 3) for flip in (False, True)}
+    partners = list(known.values()) + [sibling]
     for partner in partners:
         pl.semaphore_signal(barrier, inc=1, device_id=partner, device_id_type=MESH)
     pl.semaphore_wait(barrier, len(partners))
@@ -128,11 +132,13 @@
     def arrived(*key):
         remote(feats.at[slot(key)], feats.at[slot(key)], gather_send.at[0], arrival(key), sibling).wait_recv()
 
-    for index in range(3):
-        sends[(index, 0)].start()
+    sends[(0, 0)].start()
+    sends[(1, 0)].start()
     arrived(0, 0, 1)
-    for index in range(3):
-        sends[(index, 1)].start()
+    sends[(2, 0)].start()
+    sends[(0, 1)].start()
+    sends[(1, 1)].start()
+    sends[(2, 1)].start()
     proj_copy.wait()
 
     def unit_copy(index):
@@ -155,16 +161,18 @@
             unit_low[there, :] = (value - half.astype(F32)).astype(BF16)
             inv_norm[there, :] = inv
 
-    def three_units(first):
-        project(first, wide)
-        project(first + 1, perm)
-        normalize(first, wide)
-        unit_copy(first).start()
-        project(first + 2, wide)
-        normalize(first + 1, perm)
-        unit_copy(first + 1).start()
-        normalize(first + 2, wide)
-        unit_copy(first + 2).start()
+    def three_units(units, ready):
+        project(units[0], wide)
+        project(units[1], perm)
+        normalize(units[0], wide)
+        unit_copy(units[0]).start()
+        normalize(units[1], perm)
+        unit_copy(units[1]).start()
+        for key in ready:
+            arrived(*key)
+        project(units[2], wide)
+        normalize(units[2], wide)
+        unit_copy(units[2]).start()
 
     scale = jnp.exp(jnp.full((1, TILE), log_scale[0], F32))
     slope = scale * LOG2E
@@ -247,23 +255,22 @@
     project(0, wide)
     normalize(0, wide)
     unit_copy(0).start()
+    arrived(0, 3, 0)
+    sends[(0, 2)].start()
+    sends[(2, 2)].start()
     arrived(0, 1, 0)
+    sends[(2, 3)].start()
+    arrived(1, 0, 1)
     sends[(1, 2)].start()
-    sends[(2, 2)].start()
-    arrived(0, 3, 0)
-    sends[(2, 3)].start()
-    arrived(1, 0, 0)
-    arrived(1, 0, 1)
-    sends[(0, 2)].start()
+    sends[(0, 3)].start()
+    arrived(0, 1, 1)
     sends[(1, 3)].start()
     arrived(0, 3, 1)
-    sends[(0, 3)].start()
-    arrived(0, 1, 1)
-    three_units(1)
-    arrived(1, 3, 1)
+    three_units((2, 3, 1), [(1, 0, 0)])
+    arrived(1, 1, 1)
+    sends[(1, 4)].start()
+    arrived(1, 3, 0)
     sends[(0, 4)].start()
-    arrived(1, 1, 0)
-    sends[(1, 4)].start()
     for index in range(4):
         unit_copy(index).wait_recv()
     cosines(0, wide)
@@ -272,9 +279,9 @@
     hand_over(0)
     pair_terms(1, perm, False)
     hand_over(1)
-    for key in ((0, 2, 0), (0, 2, 1), (1, 1, 1), (1, 3, 0)):
+    for key in ((1, 3, 1), (0, 2, 0), (0, 2, 1)):
         arrived(*key)
-    three_units(4)
+    three_units((4, 6, 5), [(1, 1, 0)])
     arrived(1, 2, 0)
     arrived(1, 2, 1)
     project(7, wide)
@@ -349,17 +356,17 @@
     tangents(order[3], perm)
     scalar_start(1, scalar_finish(0))
 
-    def weights(t):
-        cols = pl.ds(pl.multiple_of(t * THIRD, PART), THIRD)
+    def weights(parts):
+        cols = pl.ds(parts[0] * PART, len(parts) * PART)
         wide[:, cols] = jnp.dot(feats_t[...], feats[:, cols], preferred_element_type=F32)
 
     up = 1 - 2 * core
 
-    def columns(t, p):
-        return pl.ds(pl.multiple_of(t * THIRD + p * PART, PART), PART)
-
-    def first_copies(t, p):
-        axis, q = ORDERS[p][0], t * 3 + p
+    def columns(q):
+        return pl.ds(q * PART, PART)
+
+    def first_copies(q):
+        axis = ORDERS[q % 3][0]
         ahead, behind = along(axis, lax.rem(4 + up, 4)), along(axis, lax.rem(4 - up, 4))
         return (
             remote(first_a.at[q], into_a.at[q], first_send.at[q, 0], first_recv.at[q, 0], ahead),
@@ -367,54 +374,56 @@
             remote(into_a.at[q], into_c.at[q], first_send.at[q, 2], first_recv.at[q, 2], ahead),
         )
 
-    def block(t, p, step):
-        k = lax.rem(pos[ORDERS[p][0]] + 4 + step, 4)
-        return pl.ds(pl.multiple_of(k * 288, 288), 288), columns(t, p)
-
-    def first_start(t, p):
+    def block(q, step):
+        k = lax.rem(pos[ORDERS[q % 3][0]] + 4 + step, 4)
+        return pl.ds(pl.multiple_of(k * 288, 288), 288), columns(q)
+
+    def first_start(q):
         for k1 in range(4):
             for k2 in range(4):
                 for k3 in range(4):
                     place = [0, 0, 0]
-                    for axis, k in zip(ORDERS[p], (k1, k2, k3)):
+                    for axis, k in zip(ORDERS[q % 3], (k1, k2, k3)):
                         place[axis] = k
-                    perm[pl.ds(k1 * 288 + k2 * 72 + k3 * 18, 18), columns(t, p)] = (
-                        wide[pl.ds(natural_row(*place), 18), columns(t, p)])
-        q = t * 3 + p
-        first_a[q] = perm[block(t, p, 2)].astype(BF16)
-        first_b[q] = perm[block(t, p, -up)].astype(BF16)
-        copies = first_copies(t, p)
+                    perm[pl.ds(k1 * 288 + k2 * 72 + k3 * 18, 18), columns(q)] = (
+                        wide[pl.ds(natural_row(*place), 18), columns(q)])
+        first_a[q] = perm[block(q, 2)].astype(BF16)
+        first_b[q] = perm[block(q, -up)].astype(BF16)
+        copies = first_copies(q)
         copies[0].start()
         copies[1].start()
 
-    def first_forward(t, p):
-        copies, q = first_copies(t, p), t * 3 + p
+    def first_forward(q):
+        copies = first_copies(q)
         copies[0].wait_recv()
-        into_a[q] = (perm[block(t, p, up)] + into_a[q].astype(F32)).astype(BF16)
+        into_a[q] = (perm[block(q, up)] + into_a[q].astype(F32)).astype(BF16)
         copies[2].start()
 
-    def second_copies(t, p):
-        q = t * 3 + p
+    def second_copies(b):
+        start, size = SECOND[b]
         return [
-            remote(second_out.at[q, step - 1], second_in.at[q, step - 1], second_send.at[q, step - 1],
-                   second_recv.at[q, step - 1], along(ORDERS[p][1], step))
+            remote(second_out.at[step - 1, pl.ds(start, size)], second_in.at[step - 1, pl.ds(start, size)],
+                   second_send.at[b, step - 1], second_recv.at[b, step - 1], known[ORDERS[BATCHES[b][0] % 3][1], step, False])
             for step in (1, 2, 3)
         ]
 
-    def second_rows(p, step):
-        return pl.ds(pl.multiple_of(lax.rem(pos[ORDERS[p][1]] + step, 4) * 72, 8), 72)
-
-    def second_start(t, p):
-        copies, q = first_copies(t, p), t * 3 + p
-        copies[1].wait_recv()
-        copies[2].wait_recv()
-        part_sum[q] = perm[block(t, p, 0)] + into_b[q].astype(F32) + into_c[q].astype(F32)
-        for step, copy in zip((1, 2, 3), second_copies(t, p)):
-            second_out[q, step - 1, pl.ds(0, 72), :] = part_sum[q, second_rows(p, step), :].astype(BF16)
+    def second_rows(q, step):
+        return pl.ds(pl.multiple_of(lax.rem(pos[ORDERS[q % 3][1]] + step, 4) * 72, 8), 72)
+
+    def second_start(b):
+        for i, q in enumerate(BATCHES[b]):
+            copies = first_copies(q)
+            copies[1].wait_recv()
+            copies[2].wait_recv()
+            part_sum[q] = perm[block(q, 0)] + into_b[q].astype(F32) + into_c[q].astype(F32)
+            for step in (1, 2, 3):
+                second_out[step - 1, pl.ds(SECOND[b][0] + 80 * i, 72), :] = part_sum[q, second_rows(q, step), :].astype(BF16)
+        for copy in second_copies(b):
             copy.start()
 
-    def third_copies(t, p):
-        axis, q = ORDERS[p][2], t * 3 + p
+    def third_copies(b):
+        axis = ORDERS[BATCHES[b][0] % 3][2]
+        rows = pl.ds(*THIRD[b])
         copies = []
         for flip in (False, True):
             half = 1 - core if flip else core
@@ -422,76 +431,67 @@
                 if step or flip:
                     sem = 3 + step if flip else step - 1
                     copies.append(remote(
-                        third_own.at[q, lax.rem(pos[axis] + step, 4), half], third_in.at[q, core, step],
-                        third_send.at[q, sem], third_recv.at[q, sem], along(axis, step, flip)))
+                        third_own.at[lax.rem(pos[axis] + step, 4), half, rows], third_in.at[core, step, rows],
+                        third_send.at[b, sem], third_recv.at[b, sem], known[axis, step, flip] if step else sibling))
         return copies
 
-    def third_start(t, p):
-        q = t * 3 + p
-        total = part_sum[q, second_rows(p, 0), :]
-        for step, copy in zip((1, 2, 3), second_copies(t, p)):
+    def third_start(b):
+        for copy in second_copies(b):
             copy.wait_recv()
-            total += second_in[q, step - 1, pl.ds(0, 72), :].astype(F32)
-        part_sum[q, pl.ds(0, 72), :] = total
-        for k in range(4):
-            for h in range(2):
-                third_own[q, k, h, pl.ds(0, 9), :] = part_sum[q, pl.ds(18 * k + 9 * h, 9), :]
-        for copy in third_copies(t, p):
+        for i, q in enumerate(BATCHES[b]):
+            total = part_sum[q, second_rows(q, 0), :]
+            for step in (1, 2, 3):
+                total += second_in[step - 1, pl.ds(SECOND[b][0] + 80 * i, 72), :].astype(F32)
+            part_sum[q, pl.ds(0, 72), :] = total
+            for k in range(4):
+                for h in range(2):
+                    third_own[k, h, pl.ds(THIRD[b][0] + 9 * i, 9), :] = part_sum[q, pl.ds(18 * k + 9 * h, 9), :]
+        for copy in third_copies(b):
             copy.start()
-        third_in[q, core, 0] = third_own[q, pos[ORDERS[p][2]], core]
-
-    def third_finish(t, p):
-        q = t * 3 + p
-        for copy in third_copies(t, p):
+        rows = pl.ds(*THIRD[b])
+        third_in[core, 0, rows] = third_own[pos[ORDERS[BATCHES[b][0] % 3][2]], core, rows]
+
+    def third_finish(b):
+        for copy in third_copies(b):
             copy.wait_recv()
-        for side in range(2):
-            got = [third_in[q, side, step, pl.ds(0, 9), :] for step in range(4)]
-            out[pl.ds(16 * side, 9), columns(t, p)] = (got[0] + got[1]) + (got[2] + got[3])
-
-    def each(step, t):
-        for p in range(3):
-            step(t, p)
-
-    def third(t, carry):
-        weights(t)
-
-        @pl.when(t > 0)
-        def _():
-            each(first_forward, t - 1)
-
-        each(first_start, t)
-
-        @pl.when(t > 1)
-        def _():
-            each(second_start, t - 2)
-
-        return carry
-
-    lax.fori_loop(0, 3, third, 0)
+        for i, q in enumerate(BATCHES[b]):
+            for side in range(2):
+                got = [third_in[side, step, pl.ds(THIRD[b][0] + 9 * i, 9), :] for step in range(4)]
+                out[pl.ds(16 * side, 9), columns(q)] = (got[0] + got[1]) + (got[2] + got[3])
+
+    def each(step, parts):
+        for q in parts:
+            step(q)
+
+    early, middle, late = range(0, 4), range(4, 7), range(7, 9)
+    weights(early)
+    each(first_start, early)
+    weights(middle)
+    each(first_start, middle)
+    each(first_forward, early)
+    weights(late)
+    each(first_start, late)
+    each(first_forward, middle)
     scalar_start(2, scalar_finish(1))
-    each(first_forward, 2)
-    each(second_start, 1)
-    each(third_start, 0)
-    each(second_start, 2)
+    each(first_forward, late)
+    each(second_start, range(0, 3))
+    each(second_start, range(3, 5))
     scalar_start(3, scalar_finish(2))
-    each(third_start, 1)
-    each(third_finish, 0)
-    each(third_start, 2)
-    each(third_finish, 1)
+    each(third_start, range(0, 3))
+    each(third_start, range(3, 5))
     totals = scalar_finish(3)
     batch = 1.0 / 16384.0
     row_scale = jnp.exp(jnp.full((8, 128), log_scale[0], F32))
     for k, value in enumerate((totals[0:8], totals[8:16] * row_scale, totals[16:24])):
         out[pl.ds(9 + k, 1), pl.ds(0, 128)] = jnp.full((1, 128), jnp.sum(value) * batch, F32)
-    each(third_finish, 2)
-
-    def sent(t, carry):
-        for p in range(3):
-            for copy in first_copies(t, p) + tuple(second_copies(t, p)) + tuple(third_copies(t, p)):
-                copy.wait_send()
-        return carry
-
-    lax.fori_loop(0, 3, sent, 0)
+    each(third_finish, range(5))
+
+    for q in range(9):
+        for copy in first_copies(q):
+            copy.wait_send()
+    for b in range(5):
+        for copy in second_copies(b) + third_copies(b):
+            copy.wait_send()
     for index in range(8):
         unit_copy(index).wait_send()
         tile_copy(index, 0, 0).wait_send()
@@ -531,17 +531,16 @@
             buffer((3, 8, TILE), F32),
             *[buffer((9, 288, PART), BF16) for _ in range(5)],
             buffer((9, 288, PART), F32),
-            buffer((9, 3, 80, PART), BF16),
-            buffer((9, 3, 80, PART), BF16),
-            buffer((9, 4, 2, 16, PART), F32),
-            buffer((9, 2, 4, 16, PART), F32),
+            buffer((3, 720, PART), BF16),
+            buffer((3, 720, PART), BF16),
+            buffer((4, 2, 112, PART), F32),
+            buffer((2, 4, 112, PART), F32),
             buffer((4, 4, 24, 128), F32),
             dma((2,)),
             dma((15,)), dma((16,)),
             dma((8,)), dma((8,)),
             dma((8,)), dma((8,)),
-            *[dma((9, 3)) for _ in range(4)],
-            dma((9, 7)), dma((9, 7)),
+            dma((9, 3)), dma((9, 3)), dma((5, 3)), dma((5, 3)), dma((5, 7)), dma((5, 7)),
             dma((10,)), dma((10,)),
         ],
         compiler_params=pltpu.CompilerParams(collective_id=0, has_side_effects=True, vmem_limit_bytes=63 * 2**20),

time: 89.3 us -> 87.5 us (0.980)
  Pallas kernels: 87 us -> 85.2 us
    pallas_call x1, Pallas kernels: 85.4 us -> 83.7 us  [per_device(): pl.pallas_call(kernel, out_shape=jax.ShapeDtypeStruct((32, WIDTH), F32),...]
where the time goes in v4:
time: 87.5 us; the launch traced here: 87.4 us
  Pallas kernels  85.2 us (97%)
  between operations  2.11 us (2%)
    pallas_call x1, Pallas kernels, per_device(): pl.pallas_call(kernel, out_shape=jax.ShapeDtypeStruct((32, WIDTH), F32),...  83.7 us

profile of v4, /device:TPU:1, one launch (start us, length us, event | category | flops | bytes accessed | tf_op | source)
XLA Modules:
  0.0 87.4 jit_solution(6082753944912507872)
XLA Ops:
  1.9 83.7 %sigmoid_loss.1.packed = f32[32,1152]{1,0:T(8,128)} custom-call(f32[1]{0:T(128)S(6)} %copy.11.log_scale, f32[1]{0:T(128)S(6)} %copy.12.logit_bias, bf16[128,1152]{1,0:T(8,128)(2,1)} %image_feats.1, bf16[128,1152]{1,0:T(8,128)(2,1)} %text_feats.1, bf16[1152,1152]{1,0:T(8,128)(2,1)} %image_proj.1, bf16[1152,1152]{1,0:T(8,128)(2,1)} %text_proj.1), custom_call_target="tpu_custom_call" | custom-call | tf_op jit(solution)/shard_map/sigmoid_loss/pallas_call | solution.py:514
  85.6 1.6 %split_outputs.1 = (f32[1]{0:T(128)}, f32[9,1152]{1,0:T(8,128)}, f32[9,1152]{1,0:T(8,128)}, f32[1]{0:T(128)}, f32[1]{0:T(128)}) custom-call(f32[32,1152]{1,0:T(8,128)} %sigmoid_loss.1.packed), custom_call_target="tpu_custom_call" | custom-call | tf_op jit(solution)/shard_map/split_outputs/pallas_call | solution.py:549

commit v5 on v4

--- a/solution.py
+++ b/solution.py
@@ -28,9 +28,9 @@
 ]
 ORDERS = [(0, 1, 2), (1, 2, 0), (2, 0, 1)]
 
-BATCHES = [(0, 3, 6), (1, 4), (2, 5), (7,), (8,)]
-SECOND = [(0, 240), (240, 160), (400, 160), (560, 80), (640, 80)]
-THIRD = [(0, 32), (32, 24), (56, 24), (80, 16), (96, 16)]
+BATCHES = [(0, 3, 6), (1, 4, 7), (2, 5), (8,)]
+SECOND = [(0, 240), (240, 240), (480, 160), (640, 80)]
+THIRD = [(0, 32), (32, 32), (64, 24), (88, 16)]
 
 
 def device(x, y, z, core):
@@ -463,7 +463,7 @@
         for q in parts:
             step(q)
 
-    early, middle, late = range(0, 4), range(4, 7), range(7, 9)
+    early, middle, late = range(0, 4), range(4, 8), range(8, 9)
     weights(early)
     each(first_start, early)
     weights(middle)
@@ -475,21 +475,21 @@
     scalar_start(2, scalar_finish(1))
     each(first_forward, late)
     each(second_start, range(0, 3))
-    each(second_start, range(3, 5))
+    each(second_start, range(3, 4))
     scalar_start(3, scalar_finish(2))
     each(third_start, range(0, 3))
-    each(third_start, range(3, 5))
+    each(third_start, range(3, 4))
     totals = scalar_finish(3)
     batch = 1.0 / 16384.0
     row_scale = jnp.exp(jnp.full((8, 128), log_scale[0], F32))
     for k, value in enumerate((totals[0:8], totals[8:16] * row_scale, totals[16:24])):
         out[pl.ds(9 + k, 1), pl.ds(0, 128)] = jnp.full((1, 128), jnp.sum(value) * batch, F32)
-    each(third_finish, range(5))
+    each(third_finish, range(4))
 
     for q in range(9):
         for copy in first_copies(q):
             copy.wait_send()
-    for b in range(5):
+    for b in range(4):
         for copy in second_copies(b) + third_copies(b):
             copy.wait_send()
     for index in range(8):
@@ -533,14 +533,14 @@
             buffer((9, 288, PART), F32),
             buffer((3, 720, PART), BF16),
             buffer((3, 720, PART), BF16),
-            buffer((4, 2, 112, PART), F32),
-            buffer((2, 4, 112, PART), F32),
+            buffer((4, 2, 104, PART), F32),
+            buffer((2, 4, 104, PART), F32),
             buffer((4, 4, 24, 128), F32),
             dma((2,)),
             dma((15,)), dma((16,)),
             dma((8,)), dma((8,)),
             dma((8,)), dma((8,)),
-            dma((9, 3)), dma((9, 3)), dma((5, 3)), dma((5, 3)), dma((5, 7)), dma((5, 7)),
+            dma((9, 3)), dma((9, 3)), dma((4, 3)), dma((4, 3)), dma((4, 7)), dma((4, 7)),
             dma((10,)), dma((10,)),
         ],
         compiler_params=pltpu.CompilerParams(collective_id=0, has_side_effects=True, vmem_limit_bytes=63 * 2**20),

time: 87.5 us -> 87.4 us (level)
  no operation moved by 1% of the time
where the time goes in v5:
time: 87.4 us; the launch traced here: 87.2 us
  Pallas kernels  85.1 us (97%)
  between operations  2.11 us (2%)
    pallas_call x1, Pallas kernels, per_device(): pl.pallas_call(kernel, out_shape=jax.ShapeDtypeStruct((32, WIDTH), F32),...  83.5 us

profile of v5, /device:TPU:1, one launch (start us, length us, event | category | flops | bytes accessed | tf_op | source)
XLA Modules:
  0.0 87.2 jit_solution(12972752245585326734)
XLA Ops:
  1.9 83.5 %sigmoid_loss.1.packed = f32[32,1152]{1,0:T(8,128)} custom-call(f32[1]{0:T(128)S(6)} %copy.11.log_scale, f32[1]{0:T(128)S(6)} %copy.12.logit_bias, bf16[128,1152]{1,0:T(8,128)(2,1)} %image_feats.1, bf16[128,1152]{1,0:T(8,128)(2,1)} %text_feats.1, bf16[1152,1152]{1,0:T(8,128)(2,1)} %image_proj.1, bf16[1152,1152]{1,0:T(8,128)(2,1)} %text_proj.1), custom_call_target="tpu_custom_call" | custom-call | tf_op jit(solution)/shard_map/sigmoid_loss/pallas_call | solution.py:514
  85.5 1.6 %split_outputs.1 = (f32[1]{0:T(128)}, f32[9,1152]{1,0:T(8,128)}, f32[9,1152]{1,0:T(8,128)}, f32[1]{0:T(128)}, f32[1]{0:T(128)}) custom-call(f32[32,1152]{1,0:T(8,128)} %sigmoid_loss.1.packed), custom_call_target="tpu_custom_call" | custom-call | tf_op jit(solution)/shard_map/split_outputs/pallas_call | solution.py:549
